TPU v7x, 512 devices: a whole 4x8x8 slice. The times are simulated.
512 devices in a mesh: seq: 128 (over x, z, y_lo), chan: 4 (over y_hi, core).
Axes of the slice: x: 4, y: 8 (y_hi: 2, y_lo: 4; y = y_hi * 4 + y_lo), z: 8, core: 2. Of those that a mesh axis runs over, the one named last changes fastest.
Arguments:
- projected: bfloat16 [3, 64, 524288], P(None, None, ('seq', 'chan')), may hold values from -6 to 6
- live_blocks: int32 [4096], P('seq'), may hold values 0 or 1
- filters: float32 [4, 524288], P('chan', 'seq'), as said below
- skip_gain: float32 [64], P('chan'), may hold values from -2 to 2
Outputs:
- gated: bfloat16 [64, 524288], P('chan', 'seq')
Inputs may be any that keep to these rules, and one draw needn't show every extreme that they name: filters holds finite float32 taps.
All inputs are finite; a program needn't handle non-finite values. No bound on the sum of `live_blocks` on one device may be relied on, other than what follows from the above.
Results may differ from a plain program's by a relative error of at most 0.0049.
Values may be sent and summed in bfloat16 or wider, within the bound.
No kernel may reach another device: no remote copies, remote signals or barrier semaphores. Data moves between devices by JAX's collectives and lax.ppermute only.
A program may use at most 128 MiB of HBM per device.

v0:
```python
from functools import partial
import math

import jax
import jax.numpy as jnp
from jax import lax
from jax.sharding import PartitionSpec as P

P_SIZE = 128
Q = 64
R = 128
N = 1048576


def unit_root(exponent, total):
    angles = 2.0 * math.pi / total * exponent.astype(jnp.float32)
    return (jnp.cos(angles), -jnp.sin(angles))


def rotate(real_part, imag_part, cos_part, sin_part):
    return (
        real_part * cos_part - imag_part * sin_part,
        real_part * sin_part + imag_part * cos_part,
    )


def dft_apply(form, mat_real, mat_imag, real_part, imag_part):
    product = partial(jnp.einsum, form, precision=lax.Precision.HIGHEST)
    if imag_part is None:
        return (product(mat_real, real_part), product(mat_imag, real_part))
    first = product(mat_real, real_part) - product(mat_imag, imag_part)
    second = product(mat_real, imag_part) + product(mat_imag, real_part)
    return (first, second)


def early_sections(real_part, imag_part, tables):
    first_real, first_imag, twist_cos, twist_sin, second_real, second_imag, outer_cos, outer_sin = (
        tables
    )
    real_part, imag_part = dft_apply("kn,cnqr->ckqr", first_real, first_imag, real_part, imag_part)
    real_part, imag_part = rotate(real_part, imag_part, twist_cos, twist_sin)
    real_part, imag_part = dft_apply(
        "kn,cpnr->cpkr", second_real, second_imag, real_part, imag_part
    )
    real_part, imag_part = rotate(real_part, imag_part, outer_cos, outer_sin)
    width_now = real_part.shape[0]
    narrow = real_part.shape[3]
    return (
        real_part.reshape(width_now, P_SIZE * Q, narrow),
        imag_part.reshape(width_now, P_SIZE * Q, narrow),
    )


def body(projected, live_blocks, filters, skip_gain):
    seq_index = lax.axis_index("seq")
    blocks = live_blocks.shape[0]
    span = blocks * R
    moved = lax.all_to_all(projected, "chan", split_axis=1, concat_axis=2, tiled=True)
    keep_rows = (
        jnp.broadcast_to(live_blocks[:, None], (blocks, R)).reshape(span).astype(jnp.float32)
    )
    gate_rows = moved[0]
    product_rows = (
        moved[1].astype(jnp.float32) * moved[2].astype(jnp.float32) * keep_rows[None, :]
    ).astype(jnp.bfloat16)
    channels = product_rows.shape[0]
    local_groups = filters.shape[0]
    half_p = P_SIZE // 2
    columns = lax.all_to_all(
        product_rows.reshape(channels, blocks, R), "seq", split_axis=2, concat_axis=1, tiled=True
    )
    narrow = columns.shape[2]
    filter_cols = lax.all_to_all(
        filters.reshape(local_groups, blocks, R), "seq", split_axis=2, concat_axis=1, tiled=True
    )
    filter_signal = filter_cols.reshape(local_groups, half_p, Q, narrow)
    signal = columns.astype(jnp.float32).reshape(channels, half_p, Q, narrow)
    real_part, imag_part = (signal, None)
    width_now = real_part.shape[0]
    first_k = jnp.arange(P_SIZE, dtype=jnp.int32)
    first_n = jnp.arange(half_p, dtype=jnp.int32)
    first_real, first_imag = unit_root(first_k[:, None] * first_n[None, :] % P_SIZE, P_SIZE)
    second_k = jnp.arange(Q, dtype=jnp.int32)
    twist_cos, twist_sin = unit_root(
        first_k[:, None] * second_k[None, :] % (P_SIZE * Q), P_SIZE * Q
    )
    twist_cos, twist_sin = (twist_cos[:, :, None], twist_sin[:, :, None])
    second_real, second_imag = unit_root(second_k[:, None] * second_k[None, :] % Q, Q)
    depth = seq_index * narrow + jnp.arange(narrow, dtype=jnp.int32)[None, None, :]
    joined = first_k[:, None, None] + P_SIZE * second_k[None, :, None]
    outer_cos, outer_sin = unit_root(joined * depth % N, N)
    tables = (
        first_real,
        first_imag,
        twist_cos,
        twist_sin,
        second_real,
        second_imag,
        outer_cos,
        outer_sin,
    )
    real_part, imag_part = early_sections(real_part, imag_part, tables)
    real_part, imag_part = (
        lax.all_to_all(real_part, "seq", split_axis=1, concat_axis=2, tiled=True),
        lax.all_to_all(imag_part, "seq", split_axis=1, concat_axis=2, tiled=True),
    )
    freq_rows = real_part.shape[1]
    filt_real, filt_imag = early_sections(filter_signal, None, tables)
    filt_real, filt_imag = (
        lax.all_to_all(filt_real, "seq", split_axis=1, concat_axis=2, tiled=True),
        lax.all_to_all(filt_imag, "seq", split_axis=1, concat_axis=2, tiled=True),
    )
    third_k = jnp.arange(R, dtype=jnp.int32)
    third_real, third_imag = unit_root(third_k[:, None] * third_k[None, :] % R, R)
    real_part, imag_part = dft_apply("kn,cfn->cfk", third_real, third_imag, real_part, imag_part)
    filt_real, filt_imag = dft_apply("kn,cfn->cfk", third_real, third_imag, filt_real, filt_imag)
    filt_real = filt_real[:, None]
    filt_imag = filt_imag[:, None]
    grouped_shape = (local_groups, width_now // local_groups, freq_rows, R)
    real_part, imag_part = rotate(
        real_part.reshape(grouped_shape), imag_part.reshape(grouped_shape), filt_real, filt_imag
    )
    real_part = real_part.reshape(width_now, freq_rows, R)
    imag_part = imag_part.reshape(width_now, freq_rows, R)
    real_part, imag_part = dft_apply("kn,cfn->cfk", third_real, -third_imag, real_part, imag_part)
    real_part, imag_part = (
        lax.all_to_all(real_part, "seq", split_axis=2, concat_axis=1, tiled=True),
        lax.all_to_all(imag_part, "seq", split_axis=2, concat_axis=1, tiled=True),
    )
    real_part = real_part.reshape(width_now, P_SIZE, Q, narrow)
    imag_part = imag_part.reshape(width_now, P_SIZE, Q, narrow)
    real_part, imag_part = rotate(real_part, imag_part, outer_cos, -outer_sin)
    real_part, imag_part = dft_apply(
        "kn,cpnr->cpkr", second_real, -second_imag, real_part, imag_part
    )
    real_part, imag_part = rotate(real_part, imag_part, twist_cos, -twist_sin)
    back_real = first_real.T
    back_imag = -first_imag.T
    product = partial(jnp.einsum, "nk,ckqr->cnqr", precision=lax.Precision.HIGHEST)
    spatial = (product(back_real, real_part) - product(back_imag, imag_part)).reshape(
        channels, half_p * Q, narrow
    )
    spatial = spatial * (1.0 / N)
    convolved = lax.all_to_all(spatial, "seq", split_axis=1, concat_axis=2, tiled=True).reshape(
        channels, span
    )
    direct = skip_gain[:, None] * product_rows.astype(jnp.float32)
    return (gate_rows.astype(jnp.float32) * (convolved + direct)).astype(jnp.bfloat16)


def solution(mesh):
    in_specs = (P(None, None, ("seq", "chan")), P("seq"), P("chan", "seq"), P("chan"))
    out_specs = P("chan", "seq")
    return jax.shard_map(body, mesh=mesh, in_specs=in_specs, out_specs=out_specs, check_vma=False)
```

profile of v0, /device:TPU:8, one launch (start us, length us, event | category | flops | bytes accessed | tf_op | source)
XLA Modules:
  0.0 653.9 jit_solution(18164930523834259752)
XLA Ops:
  1.4 17.6 %all-to-all-start.4 = ((f32[1,32,128]{1,0,2:T(1,128)}), f32[1,32,128]{1,0,2:T(1,128)S(1)}, u32[]{:S(2)}, u32[]{:S(2)}) async-start(f32[1,32,128]{1,0,2:T(1,128)} %copy.74), calls=%async_computation.4 | async-start | bytes 131072 | tf_op jit(solution)/shard_map/all_to_all | solution.py:73
  22.0 8.4 %all-to-all-done.4 = f32[1,32,128]{1,0,2:T(1,128)S(1)} async-done(((f32[1,32,128]{1,0,2:T(1,128)}), f32[1,32,128]{1,0,2:T(1,128)S(1)}, u32[]{:S(2)}, u32[]{:S(2)}) %all-to-all-start.4) | async-done | bytes 16416 | tf_op jit(solution)/shard_map/all_to_all | solution.py:73
  30.4 4.4 all-to-all-start
  36.4 16.8 %all-to-all-done = bf16[3,64,1024]{2,0,1:T(4,128)(2,1)S(1)} async-done(((bf16[3,64,1024]{2,0,1:T(4,128)(2,1)}), bf16[3,64,1024]{2,0,1:T(4,128)(2,1)S(1)}, u32[]{:S(2)}, u32[]{:S(2)}) %all-to-all-start) | async-done | bytes 393248 | tf_op jit(solution)/shard_map/all_to_all | solution.py:58
  55.3 6.3 all-to-all-start.1
  63.2 8.1 %reshape.478 = f32[1,8192,1]{2,0,1:T(1,128)} reshape(f32[128,64]{1,0:T(8,128)S(1)} %copy.77) | data formatting | bytes 65536 | tf_op jit(solution)/shard_map/reshape | solution.py:50
  71.4 8.1 %reshape.477 = f32[1,8192,1]{2,0,1:T(1,128)} reshape(f32[128,64]{1,0:T(8,128)S(1)} %copy.75) | data formatting | bytes 65536 | tf_op jit(solution)/shard_map/reshape | solution.py:49
  79.5 14.6 %all-to-all-start.6 = ((f32[1,8192,1]{2,0,1:T(1,128)}), f32[1,8192,1]{2,0,1:T(1,128)}, u32[]{:S(2)}, u32[]{:S(2)}) async-start(f32[1,8192,1]{2,0,1:T(1,128)} %reshape.478), calls=%async_computation.6 | async-start | bytes 8388608 | tf_op jit(solution)/shard_map/all_to_all | solution.py:111
  98.3 90.1 %all-to-all-done.6 = f32[1,8192,1]{2,0,1:T(1,128)} async-done(((f32[1,8192,1]{2,0,1:T(1,128)}), f32[1,8192,1]{2,0,1:T(1,128)}, u32[]{:S(2)}, u32[]{:S(2)}) %all-to-all-start.6) | async-done | bytes 32800 | tf_op jit(solution)/shard_map/all_to_all | solution.py:111
  188.4 13.1 %all-to-all-start.5 = ((f32[1,8192,1]{2,0,1:T(1,128)}), f32[1,8192,1]{2,0,1:T(1,128)}, u32[]{:S(2)}, u32[]{:S(2)}) async-start(f32[1,8192,1]{2,0,1:T(1,128)} %reshape.477), calls=%async_computation.5 | async-start | bytes 8388608 | tf_op jit(solution)/shard_map/all_to_all | solution.py:110
  202.4 4.4 copy.96
  207.4 38.4 %reduce.2 = f32[8192,16]{1,0:T(8,128)} reduce(f32[8192,1,16]{2,1,0:T(1,128)} %bitcast.222, f32[]{:T(128)} %broadcast.521), dimensions={1}, to_apply=%bitcast.191.reduce_sub_computation | reduce | bytes 1048580
  245.7 4.2 reshape.483
  249.9 46.1 %all-to-all-done.5 = f32[1,8192,1]{2,0,1:T(1,128)} async-done(((f32[1,8192,1]{2,0,1:T(1,128)}), f32[1,8192,1]{2,0,1:T(1,128)}, u32[]{:S(2)}, u32[]{:S(2)}) %all-to-all-start.5) | async-done | bytes 32800 | tf_op jit(solution)/shard_map/all_to_all | solution.py:110
  296.0 13.0 %all-to-all-start.3 = ((f32[128,1,1024]{2,1,0:T(1,128)}), f32[128,1,1024]{2,1,0:T(1,128)S(1)}, u32[]{:S(2)}, u32[]{:S(2)}) async-start(f32[128,1,1024]{2,1,0:T(1,128)} %reshape.483), calls=%async_computation.3 | async-start | bytes 1048576 | tf_op jit(solution)/shard_map/all_to_all | solution.py:105
  309.0 62.0 %reduce.1 = f32[8192]{0:T(1024)S(1)} reduce(f32[1,8192,1]{2,0,1:T(1,128)} %all-to-all-done.6, f32[]{:T(128)} %constant.86), dimensions={0,2}, to_apply=%all_to_all.134.reduce_sub_computation | reduce | bytes 65540 | tf_op jit(solution)/shard_map/all_to_all | solution.py:111
  371.0 4.4 copy.93
  375.4 38.4 %reduce.4 = f32[8192,16]{1,0:T(8,128)} reduce(f32[8192,1,16]{2,1,0:T(1,128)} %bitcast.223, f32[]{:T(128)} %broadcast.521), dimensions={1}, to_apply=%bitcast.193.reduce_sub_computation | reduce | bytes 1048580
  413.8 4.2 reshape.485
  418.0 14.6 %all-to-all-start.2 = ((f32[128,1,1024]{2,1,0:T(1,128)}), f32[128,1,1024]{2,1,0:T(1,128)S(1)}, u32[]{:S(2)}, u32[]{:S(2)}) async-start(f32[128,1,1024]{2,1,0:T(1,128)} %reshape.485), calls=%async_computation.2 | async-start | bytes 1048576 | tf_op jit(solution)/shard_map/all_to_all | solution.py:104
  433.1 62.0 %reduce = f32[8192]{0:T(1024)S(1)} reduce(f32[1,8192,1]{2,0,1:T(1,128)} %all-to-all-done.5, f32[]{:T(128)} %constant.86), dimensions={0,2}, to_apply=%all_to_all.131.reduce_sub_computation | reduce | bytes 65540 | tf_op jit(solution)/shard_map/all_to_all | solution.py:110
  498.4 9.3 %reshape.484 = f32[8192,1,16]{2,1,0:T(1,128)} reshape(f32[128,1024]{1,0:T(8,128)S(1)} %reduce.3) | data formatting | bytes 1048576
  507.7 4.1 copy.73
  514.5 9.3 %reshape.486 = f32[8192,1,16]{2,1,0:T(1,128)} reshape(f32[128,1024]{1,0:T(8,128)S(1)} %reduce.5) | data formatting | bytes 1048576
  533.8 14.1 %all-to-all-start.7 = ((f32[128,1,1024]{2,1,0:T(1,128)}), f32[128,1,1024]{2,1,0:T(1,128)S(1)}, u32[]{:S(2)}, u32[]{:S(2)}) async-start(f32[128,1,1024]{2,1,0:T(1,128)} %reshape.489), calls=%async_computation.7 | async-start | bytes 1048576 | tf_op jit(solution)/shard_map/all_to_all | solution.py:127
  551.6 12.9 %all-to-all-done.7 = f32[128,1,1024]{2,1,0:T(1,128)S(1)} async-done(((f32[128,1,1024]{2,1,0:T(1,128)}), f32[128,1,1024]{2,1,0:T(1,128)S(1)}, u32[]{:S(2)}, u32[]{:S(2)}) %all-to-all-start.7) | async-done | bytes 524320 | tf_op jit(solution)/shard_map/all_to_all | solution.py:127
  564.4 6.6 %all-to-all-start.8 = ((f32[128,1,1024]{2,1,0:T(1,128)}), f32[128,1,1024]{2,1,0:T(1,128)S(1)}, u32[]{:S(2)}, u32[]{:S(2)}) async-start(f32[128,1,1024]{2,1,0:T(1,128)} %reshape.487), calls=%async_computation.8 | async-start | bytes 1048576 | tf_op jit(solution)/shard_map/all_to_all | solution.py:128
  574.2 15.9 %all-to-all-done.8 = f32[128,1,1024]{2,1,0:T(1,128)S(1)} async-done(((f32[128,1,1024]{2,1,0:T(1,128)}), f32[128,1,1024]{2,1,0:T(1,128)S(1)}, u32[]{:S(2)}, u32[]{:S(2)}) %all-to-all-start.8) | async-done | bytes 524320 | tf_op jit(solution)/shard_map/all_to_all | solution.py:128
  602.6 19.5 %reduce.8 = f32[4096,16]{1,0:T(8,128)} reduce(f32[4096,1,16]{2,1,0:T(1,128)S(1)} %bitcast.224, f32[]{:T(128)} %broadcast.521), dimensions={1}, to_apply=%bitcast.199.reduce_sub_computation | reduce | bytes 524292
  625.1 6.6 %all-to-all-start.9 = ((f32[128,1,512]{2,1,0:T(1,128)}), f32[128,1,512]{2,1,0:T(1,128)S(1)}, u32[]{:S(2)}, u32[]{:S(2)}) async-start(f32[128,1,512]{2,1,0:T(1,128)} %reshape.491), calls=%async_computation.9 | async-start | bytes 524288 | tf_op jit(solution)/shard_map/all_to_all | solution.py:144
  634.5 11.0 %all-to-all-done.9 = f32[128,1,512]{2,1,0:T(1,128)S(1)} async-done(((f32[128,1,512]{2,1,0:T(1,128)}), f32[128,1,512]{2,1,0:T(1,128)S(1)}, u32[]{:S(2)}, u32[]{:S(2)}) %all-to-all-start.9) | async-done | bytes 262176 | tf_op jit(solution)/shard_map/all_to_all | solution.py:144
  646.7 3.9 reshape.492
  (93 shorter events, 60.9 us)
Async XLA Ops:
  1.4 29.0 %all-to-all-start.4 = ((f32[1,32,128]{1,0,2:T(1,128)}), f32[1,32,128]{1,0,2:T(1,128)S(1)}, u32[]{:S(2)}, u32[]{:S(2)}) async-start(f32[1,32,128]{1,0,2:T(1,128)} %copy.74), calls=%async_computation.4 | async-start | bytes 131072 | tf_op jit(solution)/shard_map/all_to_all | solution.py:73
  30.4 22.8 %all-to-all-start = ((bf16[3,64,1024]{2,0,1:T(4,128)(2,1)}), bf16[3,64,1024]{2,0,1:T(4,128)(2,1)S(1)}, u32[]{:S(2)}, u32[]{:S(2)}) async-start(bf16[3,64,1024]{2,0,1:T(4,128)(2,1)} %copy.60), calls=%async_computation | async-start | bytes 1048576 | tf_op jit(solution)/shard_map/all_to_all | solution.py:58
  53.6 25.9 %copy-start = (bf16[3,4,16,1024]{3,1,2,0:T(4,128)(2,1)}, bf16[3,4,16,1024]{3,1,2,0:T(4,128)(2,1)S(1)}, u32[]{:S(2)}) copy-start(bf16[3,4,16,1024]{3,1,2,0:T(4,128)(2,1)S(1)} %copy.109) | copy-start | bytes 1179652
  55.3 24.2 %all-to-all-start.1 = ((bf16[128,2,256]{2,1,0:T(2,128)(2,1)}), bf16[128,2,256]{2,1,0:T(2,128)(2,1)S(1)}, u32[]{:S(2)}, u32[]{:S(2)}) async-start(bf16[128,2,256]{2,1,0:T(2,128)(2,1)} %reshape.481), calls=%async_computation.1 | async-start | bytes 262144 | tf_op jit(solution)/shard_map/all_to_all | solution.py:69
  63.1 138.3 %copy-start.2 = (f32[128,64]{0,1:T(8,128)}, f32[128,64]{0,1:T(8,128)S(1)}, u32[]{:S(2)}) copy-start(f32[128,64]{0,1:T(8,128)S(1)} %get-tuple-element.15) | copy-start | bytes 98308
  79.5 108.9 %all-to-all-start.6 = ((f32[1,8192,1]{2,0,1:T(1,128)}), f32[1,8192,1]{2,0,1:T(1,128)}, u32[]{:S(2)}, u32[]{:S(2)}) async-start(f32[1,8192,1]{2,0,1:T(1,128)} %reshape.478), calls=%async_computation.6 | async-start | bytes 8388608 | tf_op jit(solution)/shard_map/all_to_all | solution.py:111
  188.4 107.6 %all-to-all-start.5 = ((f32[1,8192,1]{2,0,1:T(1,128)}), f32[1,8192,1]{2,0,1:T(1,128)}, u32[]{:S(2)}, u32[]{:S(2)}) async-start(f32[1,8192,1]{2,0,1:T(1,128)} %reshape.477), calls=%async_computation.5 | async-start | bytes 8388608 | tf_op jit(solution)/shard_map/all_to_all | solution.py:110
  296.0 122.0 %all-to-all-start.3 = ((f32[128,1,1024]{2,1,0:T(1,128)}), f32[128,1,1024]{2,1,0:T(1,128)S(1)}, u32[]{:S(2)}, u32[]{:S(2)}) async-start(f32[128,1,1024]{2,1,0:T(1,128)} %reshape.483), calls=%async_computation.3 | async-start | bytes 1048576 | tf_op jit(solution)/shard_map/all_to_all | solution.py:105
  418.0 94.6 %all-to-all-start.2 = ((f32[128,1,1024]{2,1,0:T(1,128)}), f32[128,1,1024]{2,1,0:T(1,128)S(1)}, u32[]{:S(2)}, u32[]{:S(2)}) async-start(f32[128,1,1024]{2,1,0:T(1,128)} %reshape.485), calls=%async_computation.2 | async-start | bytes 1048576 | tf_op jit(solution)/shard_map/all_to_all | solution.py:104
  533.8 30.6 %all-to-all-start.7 = ((f32[128,1,1024]{2,1,0:T(1,128)}), f32[128,1,1024]{2,1,0:T(1,128)S(1)}, u32[]{:S(2)}, u32[]{:S(2)}) async-start(f32[128,1,1024]{2,1,0:T(1,128)} %reshape.489), calls=%async_computation.7 | async-start | bytes 1048576 | tf_op jit(solution)/shard_map/all_to_all | solution.py:127
  547.9 23.3 %copy-start.3 = (f32[128,64]{0,1:T(8,128)S(1)}, f32[128,64]{0,1:T(8,128)}, u32[]{:S(2)}) copy-start(f32[128,64]{0,1:T(8,128)} %copy-done.2) | copy-start | bytes 98308
  547.9 23.3 %copy-start.4 = (f32[128,64]{0,1:T(8,128)S(1)}, f32[128,64]{0,1:T(8,128)}, u32[]{:S(2)}) copy-start(f32[128,64]{0,1:T(8,128)} %get-tuple-element.11) | copy-start | bytes 98308
  564.4 25.7 %all-to-all-start.8 = ((f32[128,1,1024]{2,1,0:T(1,128)}), f32[128,1,1024]{2,1,0:T(1,128)S(1)}, u32[]{:S(2)}, u32[]{:S(2)}) async-start(f32[128,1,1024]{2,1,0:T(1,128)} %reshape.487), calls=%async_computation.8 | async-start | bytes 1048576 | tf_op jit(solution)/shard_map/all_to_all | solution.py:128
  625.1 20.4 %all-to-all-start.9 = ((f32[128,1,512]{2,1,0:T(1,128)}), f32[128,1,512]{2,1,0:T(1,128)S(1)}, u32[]{:S(2)}, u32[]{:S(2)}) async-start(f32[128,1,512]{2,1,0:T(1,128)} %reshape.491), calls=%async_computation.9 | async-start | bytes 524288 | tf_op jit(solution)/shard_map/all_to_all | solution.py:144
  632.8 19.2 %copy-start.5 = (f32[16]{0:T(128)S(1)}, f32[16]{0:T(128)}, u32[]{:S(2)}) copy-start(f32[16]{0:T(128)} %param.7) | copy-start | bytes 196
  634.5 17.5 %copy-start.1 = (f32[2,8,4,1024]{3,1,2,0:T(8,128)S(1)}, f32[2,8,4,1024]{3,1,2,0:T(8,128)}, u32[]{:S(2)}) copy-start(f32[2,8,4,1024]{3,1,2,0:T(8,128)} %copy.104) | copy-start | bytes 786436
where the time goes:
time: 660 us; the launch traced here: 654 us
  other arithmetic  235 us (36%)
  waiting for transfers between devices  201 us (30%)
  starting transfers between devices  111 us (17%)
  local copies, waits for them, and re-layouts  86.3 us (13%)
  matrix products  20.1 us (3%)
    unnamed x3, other arithmetic  96.3 us
    all_to_all x1, waiting for transfers between devices, body(): lax.all_to_all(filt_imag, 'seq', split_axis=1, concat_axis=2, tiled=True)  90.1 us
    all_to_all x1, other arithmetic, body(): lax.all_to_all(filt_imag, 'seq', split_axis=1, concat_axis=2, tiled=True)  62 us
    all_to_all x1, other arithmetic, body(): lax.all_to_all(filt_real, 'seq', split_axis=1, concat_axis=2, tiled=True)  62 us
    all_to_all x1, waiting for transfers between devices, body(): lax.all_to_all(filt_real, 'seq', split_axis=1, concat_axis=2, tiled=True)  46.1 us
    unnamed x28, local copies, waits for them, and re-layouts  43 us
    all_to_all x1, starting transfers between devices, body(): lax.all_to_all(filters.reshape(local_groups, blocks, R), 'seq', split_axi...  17.6 us
    all_to_all x1, waiting for transfers between devices, body(): lax.all_to_all(projected, 'chan', split_axis=1, concat_axis=2, tiled=True)  16.8 us
  transfers between devices with their start and end apart: 10, of which 7 were waited for; matrix products, arithmetic and copies ran while one was open for 42% of the time, Pallas kernels for 0%

commit v1 on v0

v1 whole, which is shorter than its diff:
```python
from functools import partial

import jax
import jax.numpy as jnp
import ml_dtypes
import numpy as np
from jax import lax
from jax.experimental import pallas as pl
from jax.experimental.pallas import tpu as pltpu
from jax.sharding import PartitionSpec as P

BLOCK = 1024
SEQ = 128
CHAN = 4
GROUP = 16
FREQ = BLOCK // SEQ
LANES = 128
VMEM = 48 * 1024 * 1024


def wave_tables():
    k = np.arange(BLOCK, dtype=np.int64)[:, None]
    t = np.arange(BLOCK, dtype=np.int64)[None, :]
    angle = 2.0 * np.pi * ((2 * k + 1) * t % (4 * BLOCK)) / (4 * BLOCK)
    return np.stack([np.cos(angle), -np.sin(angle)]).astype(ml_dtypes.bfloat16)


def lane_ids(shape):
    return lax.broadcasted_iota(jnp.int32, shape, len(shape) - 1)


def row_ids(shape):
    return lax.broadcasted_iota(jnp.int32, shape, len(shape) - 2)


def swap_parts(v):
    is_real = (lane_ids(v.shape) // GROUP) % 2 == 0
    up = pltpu.roll(v, LANES - GROUP, 1)
    down = pltpu.roll(v, GROUP, 1)
    return jnp.where(is_real, -up, down)


def product_kernel(live_ref, proj_ref, out_ref):
    first = lax.axis_index("chan") * (BLOCK // 128)
    for part in range(BLOCK // 128):
        at = pl.ds(part * 128, 128)
        keep = live_ref[first + part].astype(jnp.float32)
        for j in range(CHAN):
            rows = pl.ds(j * GROUP, GROUP)
            key = proj_ref[1, rows, at].astype(jnp.float32)
            value = proj_ref[2, rows, at].astype(jnp.float32)
            out_ref[j, pl.ds(0, GROUP), at] = proj_ref[0, rows, at]
            out_ref[j, pl.ds(GROUP, GROUP), at] = (key * value * keep).astype(jnp.bfloat16)


def masked_product(live_blocks, projected):
    return pl.pallas_call(
        product_kernel,
        out_shape=jax.ShapeDtypeStruct((CHAN, 2 * GROUP, BLOCK), jnp.bfloat16),
        in_specs=[
            pl.BlockSpec(memory_space=pltpu.SMEM),
            pl.BlockSpec(memory_space=pltpu.VMEM),
        ],
        out_specs=pl.BlockSpec(memory_space=pltpu.VMEM),
        compiler_params=pltpu.CompilerParams(vmem_limit_bytes=VMEM),
        name="masked_product",
    )(live_blocks, projected)


FWD_TILE = 256


def forward_kernel(rows_ref, taps_ref, wave_ref, out_ref, cols):
    @pl.when(pl.program_id(0) == 0)
    def _():
        for j in range(CHAN):
            part = rows_ref[j, pl.ds(GROUP, GROUP), :].astype(jnp.float32)
            both = jnp.concatenate([part, part], axis=0)
            cols[:, pl.ds(j * 2 * GROUP, 2 * GROUP)] = both.T.astype(jnp.bfloat16)
        taps = taps_ref[...]
        high = taps.astype(jnp.bfloat16).astype(jnp.float32)
        low = taps - high
        stacked = [v[j : j + 1, :] for v in (high, low) for j in range(CHAN) for _ in (0, 1)]
        stacked.append(jnp.zeros((LANES - 4 * CHAN, BLOCK), jnp.float32))
        cols[:, pl.ds(LANES, LANES)] = jnp.concatenate(stacked, axis=0).T.astype(jnp.bfloat16)

    weights = cols[...]
    real = jnp.dot(wave_ref[0], weights, preferred_element_type=jnp.float32)
    imag = jnp.dot(wave_ref[1], weights, preferred_element_type=jnp.float32)
    lane = lane_ids((FWD_TILE, LANES))
    signal = jnp.where((lane // GROUP) % 2 == 0, real[:, :LANES], imag[:, :LANES])
    taps = jnp.where(lane % 2 == 0, real[:, LANES:], imag[:, LANES:])
    taps = taps + pltpu.roll(taps, LANES - 2 * CHAN, 1)
    high = taps.astype(jnp.bfloat16).astype(jnp.float32)
    low = pltpu.roll(taps - high, 2 * CHAN, 1)
    taps = jnp.where(lane < 2 * CHAN, high, jnp.where(lane < 4 * CHAN, low, 0.0))
    shape = (FWD_TILE // FREQ, FREQ, LANES)
    both = jnp.concatenate([signal.reshape(shape), taps.reshape(shape)], axis=1)
    out_ref[...] = both.astype(jnp.bfloat16)


def forward_blocks(rows, taps, wave):
    steps = BLOCK // FWD_TILE
    return pl.pallas_call(
        forward_kernel,
        grid=(steps,),
        out_shape=jax.ShapeDtypeStruct((SEQ, 2 * FREQ, LANES), jnp.bfloat16),
        in_specs=[
            pl.BlockSpec((CHAN, 2 * GROUP, BLOCK), lambda i: (0, 0, 0)),
            pl.BlockSpec((CHAN, BLOCK), lambda i: (0, 0)),
            pl.BlockSpec((2, FWD_TILE, BLOCK), lambda i: (0, i, 0)),
        ],
        out_specs=pl.BlockSpec((FWD_TILE // FREQ, 2 * FREQ, LANES), lambda i: (i, 0, 0)),
        scratch_shapes=[pltpu.VMEM((BLOCK, 2 * LANES), jnp.bfloat16)],
        compiler_params=pltpu.CompilerParams(vmem_limit_bytes=VMEM),
        name="forward_blocks",
    )(rows, taps, wave)


def mix_kernel(in_ref, out_ref, spread, wide, matrix):
    spread[...] = in_ref[...].astype(jnp.float32)
    square = (SEQ, LANES)
    row, lane = row_ids(square), lane_ids(square)
    comb = spread[:, FREQ, :]
    for k in range(1, FREQ):
        comb = comb + pltpu.roll(spread[:, FREQ + k, :], k * 4 * CHAN, 1)
    negate = jnp.where((row + lane) % SEQ == 0, 1.0, 0.0).astype(jnp.bfloat16)
    turned = jnp.dot(comb.T.astype(jnp.bfloat16), negate, preferred_element_type=jnp.float32)
    causal = lane <= row
    small = (2 * CHAN, SEQ)
    small_row, small_lane = row_ids(small), lane_ids(small)
    for k in range(FREQ):
        base = k * 4 * CHAN
        spec = turned[base : base + 2 * CHAN, :] + turned[base + 2 * CHAN : base + 4 * CHAN, :]
        late = jnp.where(small_lane == 0, 0.0, pltpu.roll(spec, SEQ - 1, 1))
        before = jnp.where(small_row >= 2 * CHAN - 2, late, spec)
        sign = -1.0 if k % 2 else 1.0
        spec = spec + sign * jnp.where(
            small_row % 2 == 0, -pltpu.roll(before, 1, 0), pltpu.roll(before, 3, 0)
        )
        for q in range(CHAN):
            for part in range(2):
                line = spec[2 * q + part : 2 * q + part + 1, :]
                tall = jnp.broadcast_to(line, square)
                toeplitz = pltpu.roll(tall, 0, 1, stride=1, stride_axis=0)
                toeplitz = jnp.where(causal, toeplitz, 0.0)
                matrix[pl.ds(part * SEQ, SEQ), pl.ds(q * SEQ, SEQ)] = toeplitz.astype(jnp.bfloat16)
        signal = spread[:, k, :]
        late = jnp.where(row == 0, 0.0, pltpu.roll(signal, 1, 0))
        shifted = [signal.astype(jnp.bfloat16)]
        for q in range(1, CHAN):
            move = 2 * GROUP * q
            moved = jnp.where(lane >= LANES - move, late, signal)
            shifted.append(pltpu.roll(moved, move, 1).astype(jnp.bfloat16))
        parts = jnp.dot(
            matrix[...], jnp.concatenate(shifted, axis=0), preferred_element_type=jnp.float32
        )
        wide[:, k, :] = parts[:SEQ, :] + swap_parts(parts[SEQ:, :])
    out_ref[...] = wide[...].astype(jnp.bfloat16)


def mix_blocks(received):
    return pl.pallas_call(
        mix_kernel,
        out_shape=jax.ShapeDtypeStruct((SEQ, FREQ, LANES), jnp.bfloat16),
        in_specs=[pl.BlockSpec(memory_space=pltpu.VMEM)],
        out_specs=pl.BlockSpec(memory_space=pltpu.VMEM),
        scratch_shapes=[
            pltpu.VMEM((SEQ, 2 * FREQ, LANES), jnp.float32),
            pltpu.VMEM((SEQ, FREQ, LANES), jnp.float32),
            pltpu.VMEM((2 * SEQ, CHAN * SEQ), jnp.bfloat16),
        ],
        compiler_params=pltpu.CompilerParams(vmem_limit_bytes=VMEM),
        name="mix_blocks",
    )(received)


INV_TILE = 256


def inverse_kernel(spec_ref, rows_ref, gain_ref, wave_ref, out_ref, turned):
    step = pl.program_id(0)

    @pl.when(step == 0)
    def _():
        turned[...] = spec_ref[...].astype(jnp.float32).T.astype(jnp.bfloat16)

    spec = turned[...]
    real = jnp.dot(spec, wave_ref[0], preferred_element_type=jnp.float32)
    imag = jnp.dot(spec, wave_ref[1], preferred_element_type=jnp.float32)
    gain = gain_ref[...]
    for p in range(CHAN):
        base = 2 * GROUP * p
        value = real[base : base + GROUP, :] + imag[base + GROUP : base + 2 * GROUP, :]
        value = value * (1.0 / BLOCK)
        gate = rows_ref[p, pl.ds(0, GROUP), :].astype(jnp.float32)
        direct = rows_ref[p, pl.ds(GROUP, GROUP), :].astype(jnp.float32)
        at = pl.ds(pl.multiple_of(p * BLOCK + step * INV_TILE, INV_TILE), INV_TILE)
        out_ref[:, at] = (gate * (value + gain * direct)).astype(jnp.bfloat16)


def inverse_blocks(spec, rows, gain, wave):
    steps = BLOCK // INV_TILE
    return pl.pallas_call(
        inverse_kernel,
        grid=(steps,),
        out_shape=jax.ShapeDtypeStruct((GROUP, CHAN * BLOCK), jnp.bfloat16),
        in_specs=[
            pl.BlockSpec((BLOCK, LANES), lambda i: (0, 0)),
            pl.BlockSpec((CHAN, 2 * GROUP, INV_TILE), lambda i: (0, 0, i)),
            pl.BlockSpec((GROUP, 1), lambda i: (0, 0)),
            pl.BlockSpec((2, BLOCK, INV_TILE), lambda i: (0, 0, i)),
        ],
        out_specs=pl.BlockSpec((GROUP, CHAN * BLOCK), lambda i: (0, 0)),
        scratch_shapes=[pltpu.VMEM((LANES, BLOCK), jnp.bfloat16)],
        compiler_params=pltpu.CompilerParams(vmem_limit_bytes=VMEM),
        name="inverse_blocks",
    )(spec, rows, gain, wave)


def body(projected, live_blocks, filters, skip_gain):
    exchange = partial(lax.all_to_all, split_axis=0, concat_axis=0, tiled=True)
    wave = jnp.asarray(wave_tables())
    rows = exchange(masked_product(live_blocks, projected), "chan")
    sent = forward_blocks(rows, filters.reshape(CHAN, BLOCK), wave)
    mixed = mix_blocks(exchange(sent, "seq"))
    spec = exchange(mixed, "seq").reshape(BLOCK, LANES)
    return inverse_blocks(spec, rows, skip_gain.reshape(GROUP, 1), wave)


def solution(mesh):
    in_specs = (P(None, None, ("seq", "chan")), P("seq"), P("chan", "seq"), P("chan"))
    out_specs = P("chan", "seq")
    return jax.shard_map(body, mesh=mesh, in_specs=in_specs, out_specs=out_specs, check_vma=False)
```

time: 660 us -> 91.9 us (0.14)
  other arithmetic: 235 us -> 1.4 us
  waiting for transfers between devices: 201 us -> 24.5 us
  starting transfers between devices: 111 us -> 12.8 us
  local copies, waits for them, and re-layouts: 86.3 us -> 6.64 us
  blocking collectives: 0 us -> 34.8 us
  matrix products: 20.1 us -> 0 us
  Pallas kernels: 0 us -> 11.3 us
    all_to_all x10 -> x2, waiting for transfers between devices: 201 us -> 24.5 us  [the longest x1 13.7 us: body(): spec = exchange(mixed, 'seq').reshape(BLOCK, LANES)]
    all_to_all x7 -> x0, other arithmetic: 133 us -> none  [the longest x1 62 us: body(): lax.all_to_all(filt_imag, 'seq', split_axis=1, concat_axis=2, tiled=True)]
    all_to_all x10 -> x2, starting transfers between devices: 111 us -> 12.8 us  [the longest x1 6.6 us: body(): spec = exchange(mixed, 'seq').reshape(BLOCK, LANES)]
    unnamed x3 -> x1, other arithmetic: 96.3 us -> 1.4 us
    unnamed x28 -> x11, local copies, waits for them, and re-layouts: 43 us -> 6.54 us
    all_to_all x0 -> x1, blocking collectives: none -> 34.8 us  [body(): mixed = mix_blocks(exchange(sent, 'seq'))]
    reshape x5 -> x2, local copies, waits for them, and re-layouts: 26.5 us -> 0.1 us  [the longest x1 0.08 us: body(): return inverse_blocks(spec, rows, skip_gain.reshape(GROUP, 1), wave)]
    dot_general x30 -> x0, matrix products: 20.1 us -> none  [the longest x12 8.86 us: dft_apply(): second = product(mat_real, imag_part) + product(mat_imag, real_part)]
  transfers between devices with their start and end apart: 10 -> 2, of which waited for: 7 -> 2; matrix products, arithmetic and copies ran while one was open for 42% -> 2% of each run, Pallas kernels for 0% -> 0%
where the time goes in v1:
time: 91.9 us; the launch traced here: 91.4 us
  blocking collectives  34.8 us (38%)
  waiting for transfers between devices  24.5 us (27%)
  starting transfers between devices  12.8 us (14%)
  Pallas kernels  11.3 us (12%)
  local copies, waits for them, and re-layouts  6.64 us (7%)
  other arithmetic  1.4 us (2%)
    all_to_all x1, blocking collectives, body(): mixed = mix_blocks(exchange(sent, 'seq'))  34.8 us
    all_to_all x1, waiting for transfers between devices, body(): spec = exchange(mixed, 'seq').reshape(BLOCK, LANES)  13.7 us
    all_to_all x1, waiting for transfers between devices, body(): rows = exchange(masked_product(live_blocks, projected), 'chan')  10.8 us
    all_to_all x1, starting transfers between devices, body(): spec = exchange(mixed, 'seq').reshape(BLOCK, LANES)  6.6 us
    unnamed x11, local copies, waits for them, and re-layouts  6.54 us
    all_to_all x1, starting transfers between devices, body(): rows = exchange(masked_product(live_blocks, projected), 'chan')  6.19 us
    pallas_call x1, Pallas kernels, mix_blocks(): pl.pallas_call(mix_kernel, out_shape=jax.ShapeDtypeStruct((SEQ, FREQ, LAN...  3.81 us
    pallas_call x1, Pallas kernels, forward_blocks(): pl.pallas_call(forward_kernel, grid=(steps,), out_shape=jax.ShapeDtypeStr...  3.51 us
  transfers between devices with their start and end apart: 2, of which 2 were waited for; matrix products, arithmetic and copies ran while one was open for 2% of the time, Pallas kernels for 0%

profile of v1, /device:TPU:8, one launch (start us, length us, event | category | flops | bytes accessed | tf_op | source)
XLA Modules:
  0.0 91.4 jit_solution(4497779650117064246)
XLA Ops:
  0.0 0.0 copy-start.2
  0.0 1.0 %copy-done.2 = bf16[3,64,1024]{2,1,0:T(8,128)(2,1)S(1)} copy-done((bf16[3,64,1024]{2,1,0:T(8,128)(2,1)S(1)}, bf16[3,64,1024]{2,1,0:T(8,128)(2,1)}, u32[]{:S(2)}) %copy-start.2) | copy-done | bytes 393240
  1.0 0.0 copy-start.3
  1.0 0.7 copy-done.3
  1.7 0.0 copy-start.4
  1.7 1.3 %masked_product.1 = bf16[4,32,1024]{2,1,0:T(8,128)(2,1)} custom-call(s32[32]{0:T(128)S(1)} %copy-done.3, bf16[3,64,1024]{2,1,0:T(8,128)(2,1)S(1)} %copy-done.2), custom_call_target="tpu_custom_call" | custom-call | tf_op jit(solution)/shard_map/masked_product/pallas_call | solution.py:57
  2.9 6.2 %all-to-all-start = ((bf16[4,32,1024]{2,1,0:T(8,128)(2,1)}), bf16[4,32,1024]{2,1,0:T(8,128)(2,1)S(1)}, u32[]{:S(2)}, u32[]{:S(2)}) async-start(bf16[4,32,1024]{2,1,0:T(8,128)(2,1)} %masked_product.1), calls=%async_computation | async-start | bytes 524288 | tf_op jit(solution)/shard_map/all_to_all | solution.py:224
  9.1 0.5 broadcast.3
  9.7 1.4 %reduce.3 = f32[4096]{0:T(1024)S(1)} reduce(f32[1,4096]{1,0:T(1,128)} %param.7, f32[]{:T(128)} %broadcast.3), dimensions={0}, to_apply=%param.7.reduce_sub_computation.3 | reduce | bytes 32772 | tf_op args[2]
  11.1 10.8 %all-to-all-done.rows_ref = bf16[4,32,1024]{2,1,0:T(8,128)(2,1)S(1)} async-done(((bf16[4,32,1024]{2,1,0:T(8,128)(2,1)}), bf16[4,32,1024]{2,1,0:T(8,128)(2,1)S(1)}, u32[]{:S(2)}, u32[]{:S(2)}) %all-to-all-start) | async-done | bytes 262176 | tf_op jit(solution)/shard_map/all_to_all | solution.py:224
  21.9 0.0 copy-start
  21.9 2.2 %copy-done = bf16[2,1024,1024]{2,1,0:T(8,128)(2,1)S(1)} copy-done((bf16[2,1024,1024]{2,1,0:T(8,128)(2,1)S(1)}, bf16[2,1024,1024]{2,1,0:T(8,128)(2,1)}, u32[]{:S(2)}) %copy-start) | copy-done | bytes 4194328
  24.1 3.5 %forward_blocks.1 = bf16[128,16,128]{2,1,0:T(8,128)(2,1)S(1)} custom-call(bf16[4,32,1024]{2,1,0:T(8,128)(2,1)S(1)} %all-to-all-done.rows_ref, f32[4,1024]{1,0:T(4,128)S(1)} %reshape.9.taps_ref, bf16[2,1024,1024]{2,1,0:T(8,128)(2,1)S(1)} %copy-done), custom_call_target="tpu_custom_call" | custom-call | tf_op jit(solution)/shard_map/forward_blocks/pallas_call | solution.py:104
  27.6 34.8 %all_to_all.15.in_ref = bf16[128,16,128]{2,1,0:T(8,128)(2,1)S(1)} all-to-all(bf16[128,16,128]{2,1,0:T(8,128)(2,1)S(1)} %forward_blocks.1), channel_id=1, replica_groups=mesh['seq'=128,'chan'=4] {'seq'}, dimensions={0} | all-to-all | bytes 1048576 | tf_op jit(solution)/shard_map/all_to_all | solution.py:226
  62.4 3.8 %mix_blocks.1 = bf16[128,8,128]{2,1,0:T(8,128)(2,1)} custom-call(bf16[128,16,128]{2,1,0:T(8,128)(2,1)S(1)} %all_to_all.15.in_ref), custom_call_target="tpu_custom_call" | custom-call | tf_op jit(solution)/shard_map/mix_blocks/pallas_call | solution.py:163
  66.2 6.6 %all-to-all-start.2 = ((bf16[128,8,128]{2,1,0:T(8,128)(2,1)}), bf16[128,8,128]{2,1,0:T(8,128)(2,1)S(1)}, u32[]{:S(2)}, u32[]{:S(2)}) async-start(bf16[128,8,128]{2,1,0:T(8,128)(2,1)} %mix_blocks.1), calls=%async_computation.2 | async-start | bytes 524288 | tf_op jit(solution)/shard_map/all_to_all | solution.py:227
  72.8 0.0 copy-done.4
  72.8 0.1 copy.6.gain_ref
  72.9 13.7 %all-to-all-done.2 = bf16[128,8,128]{2,1,0:T(8,128)(2,1)S(1)} async-done(((bf16[128,8,128]{2,1,0:T(8,128)(2,1)}), bf16[128,8,128]{2,1,0:T(8,128)(2,1)S(1)}, u32[]{:S(2)}, u32[]{:S(2)}) %all-to-all-start.2) | async-done | bytes 262176 | tf_op jit(solution)/shard_map/all_to_all | solution.py:227
  86.5 0.0 copy-start.1
  86.6 2.2 %copy-done.1 = bf16[2,1024,1024]{2,1,0:T(8,128)(2,1)S(1)} copy-done((bf16[2,1024,1024]{2,1,0:T(8,128)(2,1)S(1)}, bf16[2,1024,1024]{2,1,0:T(8,128)(2,1)}, u32[]{:S(2)}) %copy-start.1) | copy-done | bytes 4194328
  88.7 2.7 %inverse_blocks.1 = bf16[16,4096]{1,0:T(8,128)(2,1)} custom-call(bf16[1024,128]{1,0:T(8,128)(2,1)S(1)} %bitcast.2, bf16[4,32,1024]{2,1,0:T(8,128)(2,1)S(1)} %all-to-all-done.rows_ref, f32[16,1]{1,0:T(8,128)S(1)} %copy.6.gain_ref, bf16[2,1024,1024]{2,1,0:T(8,128)(2,1)S(1)} %copy-done.1), custom_call_target="tpu_custom_call" | custom-call | tf_op jit(solution)/shard_map/inverse_blocks/pallas_call | solution.py:204
  (1 shorter events, 0.0 us)
Async XLA Ops:
  0.0 1.0 %copy-start.2 = (bf16[3,64,1024]{2,1,0:T(8,128)(2,1)S(1)}, bf16[3,64,1024]{2,1,0:T(8,128)(2,1)}, u32[]{:S(2)}) copy-start(bf16[3,64,1024]{2,1,0:T(8,128)(2,1)} %proj_ref.1) | copy-start | bytes 1179652
  1.0 0.7 copy-start.3
  1.7 71.2 %copy-start.4 = (f32[16]{0:T(128)S(1)}, f32[16]{0:T(128)}, u32[]{:S(2)}) copy-start(f32[16]{0:T(128)} %param.8) | copy-start | bytes 196
  2.9 18.9 %all-to-all-start = ((bf16[4,32,1024]{2,1,0:T(8,128)(2,1)}), bf16[4,32,1024]{2,1,0:T(8,128)(2,1)S(1)}, u32[]{:S(2)}, u32[]{:S(2)}) async-start(bf16[4,32,1024]{2,1,0:T(8,128)(2,1)} %masked_product.1), calls=%async_computation | async-start | bytes 524288 | tf_op jit(solution)/shard_map/all_to_all | solution.py:224
  21.9 2.2 %copy-start = (bf16[2,1024,1024]{2,1,0:T(8,128)(2,1)S(1)}, bf16[2,1024,1024]{2,1,0:T(8,128)(2,1)}, u32[]{:S(2)}) copy-start(bf16[2,1024,1024]{2,1,0:T(8,128)(2,1)} %constant.2.clone.wave_ref) | copy-start | bytes 12582916
  66.2 20.4 %all-to-all-start.2 = ((bf16[128,8,128]{2,1,0:T(8,128)(2,1)}), bf16[128,8,128]{2,1,0:T(8,128)(2,1)S(1)}, u32[]{:S(2)}, u32[]{:S(2)}) async-start(bf16[128,8,128]{2,1,0:T(8,128)(2,1)} %mix_blocks.1), calls=%async_computation.2 | async-start | bytes 524288 | tf_op jit(solution)/shard_map/all_to_all | solution.py:227
  86.5 2.2 %copy-start.1 = (bf16[2,1024,1024]{2,1,0:T(8,128)(2,1)S(1)}, bf16[2,1024,1024]{2,1,0:T(8,128)(2,1)}, u32[]{:S(2)}) copy-start(bf16[2,1024,1024]{2,1,0:T(8,128)(2,1)} %constant.2.clone.wave_ref) | copy-start | bytes 12582916

commit v2 on v1

v2 whole, which is shorter than its diff:
```python
from functools import partial

import jax
import jax.numpy as jnp
import ml_dtypes
import numpy as np
from jax import lax
from jax.experimental import pallas as pl
from jax.experimental.pallas import tpu as pltpu
from jax.sharding import Mesh, PartitionSpec as P

BLOCK = 1024
SEQ = 128
CHAN = 4
GROUP = 16
FREQ = BLOCK // SEQ
LANES = 128
HALF = 64
SIGNAL = 4
MESSAGE = 6
PAIR = 2 * MESSAGE
MIB = 1024 * 1024
COST = pl.CostEstimate(flops=6_000_000_000, bytes_accessed=20_000_000, transcendentals=0)
ON_CHIP = pl.BlockSpec(memory_space=pltpu.VMEM)


BASE = BLOCK // 2
QUAD = FREQ // 2


def wave_tables():
    k = np.arange(BASE, dtype=np.int64).reshape(SEQ, QUAD).T.reshape(BASE, 1)
    t = np.arange(BLOCK, dtype=np.int64)[None, :]
    angle = 2.0 * np.pi * ((2 * k + 1) * t % (4 * BLOCK)) / (4 * BLOCK)
    return np.stack([np.cos(angle), -np.sin(angle)]).astype(ml_dtypes.bfloat16)


def lane_ids(shape):
    return lax.broadcasted_iota(jnp.int32, shape, len(shape) - 1)


def row_ids(shape):
    return lax.broadcasted_iota(jnp.int32, shape, len(shape) - 2)


def swap_parts(v):
    is_real = (lane_ids(v.shape) // GROUP) % 2 == 0
    up = pltpu.roll(v, LANES - GROUP, 1)
    down = pltpu.roll(v, GROUP, 1)
    return jnp.where(is_real, -up, down)


def gain_kernel(gain_ref, out_ref):
    out_ref[...] = jnp.concatenate([gain_ref[...]] * (LANES // GROUP), axis=1)


def lane_gains(skip_gain):
    return pl.pallas_call(
        gain_kernel,
        out_shape=jax.ShapeDtypeStruct((1, LANES), jnp.float32),
        in_specs=[ON_CHIP],
        out_specs=ON_CHIP,
        compiler_params=pltpu.CompilerParams(vmem_limit_bytes=60 * MIB),
        cost_estimate=COST,
        name="lane_gains",
    )(skip_gain.reshape(1, GROUP))


def forward_kernel(
    live_ref, own_ref, got_ref, taps_ref, wave, out_ref, gate_ref, send_ref, cols, packed
):
    high, core = lax.axis_index("yh"), lax.axis_index("core")
    count = 4 * GROUP
    piece = (GROUP, LANES)
    even = lane_ids(piece) % 2 == 0
    for part in range(2):
        rows = pl.ds(pl.multiple_of((2 * part + core) * GROUP, GROUP), GROUP)
        for blk in range(2):

            def read(i, at):
                return jnp.where(core == blk, own_ref[i, rows, at], got_ref[i, rows, at])

            to = (2 * part + blk) * GROUP
            for block in range(BLOCK // LANES):
                at = pl.ds(block * LANES, LANES)
                live = live_ref[(2 * high + blk) * (BLOCK // LANES) + block].astype(jnp.float32)
                key, value = read(1, at).astype(jnp.float32), read(2, at).astype(jnp.float32)
                value = key * value * live
                cols[pl.ds(to, GROUP), at] = jnp.where(even, value, 0.0).astype(jnp.bfloat16)
                cols[pl.ds(count + to, GROUP), at] = jnp.where(even, 0.0, value).astype(
                    jnp.bfloat16
                )
            gate = read(0, slice(None))

            @pl.when(high == part)
            def _():
                gate_ref[blk] = gate

            @pl.when(high != part)
            def _():
                send_ref[blk] = gate

    even = lane_ids((GROUP, BLOCK)) % 2 == 0
    taps = jnp.concatenate(
        [taps_ref[:, j * BLOCK : (j + 1) * BLOCK] for j in range(CHAN)], axis=0
    )
    top = taps.astype(jnp.bfloat16).astype(jnp.float32)
    taps = jnp.concatenate([top, taps - top, top, taps - top], axis=0)
    kept = even == (row_ids((GROUP, BLOCK)) < 2 * CHAN)
    cols[pl.ds(LANES, GROUP), :] = jnp.where(kept, taps, 0.0).astype(jnp.bfloat16)
    cols[pl.ds(LANES + GROUP, LANES - GROUP), :] = jnp.zeros(
        (LANES - GROUP, BLOCK), jnp.bfloat16
    )
    weights = cols[...]
    sums = []
    for i in range(2):
        sums.append(
            lax.dot_general(
                wave[i], weights, (((1,), (1,)), ((), ())), preferred_element_type=jnp.float32
            )
        )

    def put(row, value):
        packed[pl.ds(row, SEQ, stride=PAIR), :] = value

    square = (SEQ, LANES)
    lane = lane_ids(square)
    comb = jnp.zeros(square, jnp.float32)
    for i in range(QUAD):
        at = slice(i * SEQ, (i + 1) * SEQ)
        cos, sin = sums[0][at, :LANES], sums[1][at, :LANES]
        turn_cos, turn_sin = pltpu.roll(cos, HALF, 1), pltpu.roll(sin, HALF, 1)
        real = jnp.where(lane < HALF, cos + turn_cos, turn_cos - cos)
        imag = jnp.where(lane < HALF, sin + turn_sin, sin - turn_sin)
        place = (lane % HALF) // GROUP
        middle = pltpu.roll(jnp.where(place == 0, imag, real), GROUP, 1)
        last = pltpu.roll(imag, 2 * GROUP, 1)
        put(i, jnp.where(place == 0, real, jnp.where(place == 3, last, middle)))
        middle = pltpu.roll(jnp.where(place == 2, imag, real), LANES - GROUP, 1)
        last = pltpu.roll(real, LANES - 2 * GROUP, 1)
        put(MESSAGE + i, jnp.where(place == 3, imag, jnp.where(place == 0, last, middle)))
        for part in range(2):
            move = part * HALF + i * GROUP
            value = sums[part][at, LANES:]
            comb = comb + (pltpu.roll(value, move, 1) if move else value)
    step = 2 * CHAN
    difference = pltpu.roll(comb, step, 1) - comb
    difference = jnp.where(lane < HALF, difference, -difference)
    both = comb + pltpu.roll(comb, LANES - step, 1)
    comb = jnp.where((lane // step) % 2 == 0, both, difference)
    comb = comb + pltpu.roll(comb, LANES - CHAN, 1)
    top = comb.astype(jnp.bfloat16).astype(jnp.float32)
    comb = jnp.where((lane // CHAN) % 2 == 0, top, pltpu.roll(comb - top, CHAN, 1))
    put(SIGNAL, jnp.where(high == 0, comb, 0.0))
    put(MESSAGE + SIGNAL, jnp.where(high == 1, comb, 0.0))
    empty = jnp.zeros(square, jnp.float32)
    put(SIGNAL + 1, empty)
    put(MESSAGE + SIGNAL + 1, empty)
    out_ref[...] = packed[...].astype(jnp.bfloat16)


def forward_blocks(live_blocks, own, got, taps, wave):
    gate = jax.ShapeDtypeStruct((2, GROUP, BLOCK), jnp.bfloat16)
    return pl.pallas_call(
        forward_kernel,
        out_shape=[jax.ShapeDtypeStruct((SEQ * PAIR, LANES), jnp.bfloat16), gate, gate],
        in_specs=[pl.BlockSpec(memory_space=pltpu.SMEM)] + [ON_CHIP] * 4,
        out_specs=[ON_CHIP] * 3,
        scratch_shapes=[
            pltpu.VMEM((2 * LANES, BLOCK), jnp.bfloat16),
            pltpu.VMEM((SEQ * PAIR, LANES), jnp.float32),
        ],
        compiler_params=pltpu.CompilerParams(vmem_limit_bytes=48 * MIB),
        name="forward_blocks",
    )(live_blocks, own, got, taps, wave)


def mix_kernel(in_ref, gain_ref, out_ref, spread, wide, matrix):
    spread[...] = in_ref[...].astype(jnp.float32)
    square = (SEQ, LANES)
    row, lane = row_ids(square), lane_ids(square)

    def take(at):
        return spread[pl.ds(at, SEQ, stride=PAIR), :]

    comb = take(SIGNAL) + take(MESSAGE + SIGNAL)
    negate = jnp.where((row + lane) % SEQ == 0, 1.0, 0.0).astype(jnp.bfloat16)
    turned = jnp.dot(comb.T.astype(jnp.bfloat16), negate, preferred_element_type=jnp.float32)
    turned = turned + pltpu.roll(turned, LANES - CHAN, 0)
    late = jnp.where(lane == 0, 0.0, pltpu.roll(turned, SEQ - 1, 1))
    before = jnp.where(
        row % CHAN == 0, pltpu.roll(late, LANES - CHAN + 1, 0), pltpu.roll(turned, 1, 0)
    )
    half_row = row_ids((HALF, LANES))
    flip = (half_row // (4 * CHAN) + half_row // (2 * CHAN)) % 2 == 1
    before = jnp.where(jnp.concatenate([flip, flip], axis=0), -before, before)
    spec = (turned[:HALF] - before[HALF:], turned[HALF:] + before[:HALF])
    causal = lane <= row
    gain = gain_ref[...]
    is_real = (lane // GROUP) % 2 == 0
    for k in range(FREQ):
        digit, mirror = k // 2, k % 2
        base = digit * 4 * CHAN + mirror * 2 * CHAN
        for q in range(CHAN):
            for part in range(2):
                line = spec[part][base + q : base + q + 1, :]
                tall = jnp.broadcast_to(line, square)
                toeplitz = pltpu.roll(tall, 0, 1, stride=1, stride_axis=0)
                toeplitz = jnp.where(causal, toeplitz, 0.0)
                matrix[pl.ds(part * SEQ, SEQ), pl.ds(q * SEQ, SEQ)] = toeplitz.astype(jnp.bfloat16)
        low, high = take(digit), take(MESSAGE + digit)
        if mirror == 0:
            signal = jnp.where(lane < HALF, low, pltpu.roll(high, HALF, 1))
        else:
            signal = jnp.where(lane < HALF, pltpu.roll(low, HALF, 1), high)
        late = jnp.where(row == 0, 0.0, pltpu.roll(signal, 1, 0))
        shifted = [signal.astype(jnp.bfloat16)]
        for q in range(1, CHAN):
            move = 2 * GROUP * q
            moved = jnp.where(lane >= LANES - move, late, signal)
            shifted.append(pltpu.roll(moved, move, 1).astype(jnp.bfloat16))
        parts = jnp.dot(
            matrix[...], jnp.concatenate(shifted, axis=0), preferred_element_type=jnp.float32
        )
        mixed = parts[:SEQ, :] + swap_parts(parts[SEQ:, :]) + gain * signal
        if mirror == 0:
            first = mixed
            continue
        plus, minus = first + mixed, first - mixed
        wide[:, digit, :] = jnp.where(is_real, plus, minus)
        wide[:, QUAD + digit, :] = jnp.where(is_real, minus, plus)
    out_ref[...] = wide[...].astype(jnp.bfloat16)


def mix_blocks(received, gain):
    return pl.pallas_call(
        mix_kernel,
        out_shape=jax.ShapeDtypeStruct((SEQ, FREQ, LANES), jnp.bfloat16),
        in_specs=[ON_CHIP, ON_CHIP],
        out_specs=ON_CHIP,
        scratch_shapes=[
            pltpu.VMEM((SEQ * PAIR, LANES), jnp.float32),
            pltpu.VMEM((SEQ, FREQ, LANES), jnp.float32),
            pltpu.VMEM((2 * SEQ, CHAN * SEQ), jnp.bfloat16),
        ],
        compiler_params=pltpu.CompilerParams(vmem_limit_bytes=48 * MIB),
        cost_estimate=COST,
        name="mix_blocks",
    )(received, gain)


def inverse_kernel(spec_ref, gate_ref, other_ref, wave, out_ref, plain):
    plain[...] = spec_ref[...].astype(jnp.float32)
    sides = [
        [plain[pl.ds(part * QUAD + i, SEQ, stride=FREQ), :].T for i in range(QUAD)]
        for part in range(2)
    ]
    sides = [jnp.concatenate(side, axis=1).astype(jnp.bfloat16) for side in sides]
    total = None
    for part in range(2):
        lines = [
            side[(2 * p + part) * GROUP : (2 * p + part + 1) * GROUP, :]
            for side in sides
            for p in range(CHAN)
        ]
        term = jnp.dot(
            jnp.concatenate(lines, axis=0), wave[part], preferred_element_type=jnp.float32
        )
        total = term if total is None else total + term
    high = lax.axis_index("yh")
    even = lane_ids((GROUP, BLOCK)) % 2 == 0
    for p in range(CHAN):
        at = p * GROUP
        value = jnp.where(
            even, total[at : at + GROUP, :], total[HALF + at : HALF + at + GROUP, :]
        )
        gate = jnp.where(high == p // 2, gate_ref[p % 2], other_ref[p % 2]).astype(jnp.float32)
        out_ref[:, pl.ds(p * BLOCK, BLOCK)] = (gate * (value * (1.0 / BLOCK))).astype(jnp.bfloat16)


def inverse_blocks(spec, gate, other, wave):
    return pl.pallas_call(
        inverse_kernel,
        out_shape=jax.ShapeDtypeStruct((GROUP, CHAN * BLOCK), jnp.bfloat16),
        in_specs=[ON_CHIP] * 4,
        out_specs=ON_CHIP,
        scratch_shapes=[pltpu.VMEM((BLOCK, LANES), jnp.float32)],
        compiler_params=pltpu.CompilerParams(vmem_limit_bytes=48 * MIB),
        name="inverse_blocks",
    )(spec, gate, other, wave)


def body(projected, live_blocks, filters, skip_gain):
    exchange = partial(lax.all_to_all, split_axis=0, concat_axis=0, tiled=True)
    wave = jnp.asarray(wave_tables())
    swap = ((0, 1), (1, 0))
    got = lax.ppermute(projected, "core", swap)
    got, gain = lax.optimization_barrier((got, lane_gains(skip_gain)))
    sent, gate, send = forward_blocks(live_blocks, projected, got, filters, wave)
    other = lax.ppermute(send, "yh", swap)
    got_spec = exchange(sent.reshape(-1, 2, LANES), ("seq", "yh")).reshape(-1, LANES)
    mixed = mix_blocks(got_spec, gain)
    spec = exchange(mixed, "seq").reshape(BLOCK, LANES)
    return inverse_blocks(spec, gate, other, wave)


def solution(mesh):
    split = Mesh(mesh.devices.reshape(SEQ, 2, 2), ("seq", "yh", "core"))
    chan = ("yh", "core")
    in_specs = (P(None, None, ("seq", "yh", "core")), P("seq"), P(chan, "seq"), P(chan))
    out_specs = P(chan, "seq")
    return jax.shard_map(body, mesh=split, in_specs=in_specs, out_specs=out_specs, check_vma=False)
```

time: 91.9 us -> 70.9 us (0.77)
  the two profiles are of different devices: /device:TPU:8 before, /device:TPU:2 now
where the time goes in v2:
time: 70.9 us; the launch traced here: 70.6 us
  blocking collectives  40.3 us (57%)
  starting transfers between devices  13.1 us (18%)
  waiting for transfers between devices  9.18 us (13%)
  Pallas kernels  7.94 us (11%)
    all_to_all x1, blocking collectives, body(): exchange(sent.reshape(-1, 2, LANES), ('seq', 'yh')).reshape(-1, LANES)  40.3 us
    all_to_all x1, starting transfers between devices, body(): spec = exchange(mixed, 'seq').reshape(BLOCK, LANES)  6.79 us
    ppermute x1, waiting for transfers between devices, body(): other = lax.ppermute(send, 'yh', swap)  6.29 us
    ppermute x1, starting transfers between devices, body(): other = lax.ppermute(send, 'yh', swap)  4.37 us
    pallas_call x1, Pallas kernels, mix_blocks(): pl.pallas_call(mix_kernel, out_shape=jax.ShapeDtypeStruct((SEQ, FREQ, LAN...  3.3 us
    all_to_all x1, waiting for transfers between devices, body(): spec = exchange(mixed, 'seq').reshape(BLOCK, LANES)  2.43 us
    pallas_call x1, Pallas kernels, forward_blocks(): pl.pallas_call(forward_kernel, out_shape=[jax.ShapeDtypeStruct((SEQ * PAI...  2.04 us
    ppermute x1, starting transfers between devices, body(): got = lax.ppermute(projected, 'core', swap)  1.91 us
  transfers between devices with their start and end apart: 3, of which 3 were waited for; matrix products, arithmetic and copies ran while one was open for 0% of the time, Pallas kernels for 2%

profile of v2, /device:TPU:2, one launch (start us, length us, event | category | flops | bytes accessed | tf_op | source)
XLA Modules:
  0.0 70.6 jit_solution(17775772947276690977)
XLA Ops:
  0.0 1.9 %collective-permute-start = (bf16[3,64,1024]{2,1,0:T(8,128)(2,1)}, bf16[3,64,1024]{2,1,0:T(8,128)(2,1)S(1)}, u32[]{:S(2)}, u32[]{:S(2)}) collective-permute-start(bf16[3,64,1024]{2,1,0:T(8,128)(2,1)} %own_ref.1), channel_id=1, source_target_pairs={{0,1},{1,0},{2,3},{3,2},{4,5},{5,4},{6,7},{7,6},{8,9},{9,8},{10,11... | collective-permute-start | bytes 1179656 | tf_op jit(solution)/shard_map/ppermute | solution.py:297
  1.9 0.0 copy-start
  1.9 0.0 copy-start.1
  1.9 0.0 copy-start.2
  1.9 0.0 copy-start.3
  2.0 1.4 %lane_gains.1.gain_ref = f32[1,128]{1,0:T(1,128)} custom-call(f32[1,16]{1,0:T(1,128)} %bitcast.7), custom_call_target="tpu_custom_call" | custom-call | flops 6000000000 | bytes 20000000 | tf_op jit(solution)/shard_map/lane_gains/pallas_call | solution.py:58
  3.4 0.0 copy-start.4
  3.4 0.5 collective-permute-done.got_ref
  3.8 0.0 copy-done
  3.8 0.0 copy-done.1
  3.8 0.0 copy-done.2
  3.8 0.0 copy-done.3
  3.8 2.0 %forward_blocks.1 = (bf16[1536,128]{1,0:T(8,128)(2,1)S(1)}, bf16[2,16,1024]{2,1,0:T(8,128)(2,1)S(1)}, bf16[2,16,1024]{2,1,0:T(8,128)(2,1)S(1)}) custom-call(s32[32]{0:T(128)S(1)} %copy-done.3, bf16[3,64,1024]{2,1,0:T(8,128)(2,1)S(1)} %copy-done.1, bf16[3,64,1024]{2,1,0:T(8,128)(2,1)S(1)} %collective-permute-done.got_ref, f32[1,4096]{1,0:T(1,128)S(1)} %copy-done.2, ...), custom_call_target="tpu_custom_call" | custom-call | tf_op jit(solution)/shard_map/forward_blocks/pallas_call | solution.py:164
  5.9 40.3 %all_to_all.10 = bf16[768,2,128]{2,1,0:T(2,128)(2,1)S(1)} all-to-all(bf16[768,2,128]{2,1,0:T(2,128)(2,1)S(1)} %bitcast.5), channel_id=1, replica_groups=mesh['seq'=128,'yh'=2,'core'=2] {'seq','yh'}, dimensions={0} | all-to-all | bytes 786432 | tf_op jit(solution)/shard_map/all_to_all | solution.py:301
  46.2 0.0 copy-done.4
  46.2 3.3 %mix_blocks.1 = bf16[128,8,128]{2,1,0:T(8,128)(2,1)} custom-call(bf16[1536,128]{1,0:T(8,128)(2,1)S(1)} %bitcast.6, f32[1,128]{1,0:T(1,128)S(1)} %copy-done.4), custom_call_target="tpu_custom_call" | custom-call | flops 6000000000 | bytes 20000000 | tf_op jit(solution)/shard_map/mix_blocks/pallas_call | solution.py:236
  49.5 6.8 %all-to-all-start.1 = ((bf16[128,8,128]{2,1,0:T(8,128)(2,1)}), bf16[128,8,128]{2,1,0:T(8,128)(2,1)S(1)}, u32[]{:S(2)}, u32[]{:S(2)}) async-start(bf16[128,8,128]{2,1,0:T(8,128)(2,1)} %mix_blocks.1), calls=%async_computation.1 | async-start | bytes 524288 | tf_op jit(solution)/shard_map/all_to_all | solution.py:303
  56.3 4.4 %collective-permute-start.1 = (bf16[2,16,1024]{2,1,0:T(8,128)(2,1)S(1)}, bf16[2,16,1024]{2,1,0:T(8,128)(2,1)S(1)}, u32[]{:S(2)}, u32[]{:S(2)}) collective-permute-start(bf16[2,16,1024]{2,1,0:T(8,128)(2,1)S(1)} %get-tuple-element.14), channel_id=1, source_target_pairs={{0,2},{2,0},{1,3},{3,1},{4,6},{6,4},{5,7},{7,5},{8,10},{10,8},{9,1... | collective-permute-start | bytes 196616 | tf_op jit(solution)/shard_map/ppermute | solution.py:300
  60.7 6.3 %collective-permute-done.1.other_ref = bf16[2,16,1024]{2,1,0:T(8,128)(2,1)S(1)} collective-permute-done((bf16[2,16,1024]{2,1,0:T(8,128)(2,1)S(1)}, bf16[2,16,1024]{2,1,0:T(8,128)(2,1)S(1)}, u32[]{:S(2)}, u32[]{:S(2)}) %collective-permute-start.1) | collective-permute-done | bytes 65568 | tf_op jit(solution)/shard_map/ppermute | solution.py:300
  66.9 2.4 %all-to-all-done.1 = bf16[128,8,128]{2,1,0:T(8,128)(2,1)S(1)} async-done(((bf16[128,8,128]{2,1,0:T(8,128)(2,1)}), bf16[128,8,128]{2,1,0:T(8,128)(2,1)S(1)}, u32[]{:S(2)}, u32[]{:S(2)}) %all-to-all-start.1) | async-done | bytes 262176 | tf_op jit(solution)/shard_map/all_to_all | solution.py:303
  69.4 1.2 %inverse_blocks.1 = bf16[16,4096]{1,0:T(8,128)(2,1)} custom-call(bf16[1024,128]{1,0:T(8,128)(2,1)S(1)} %bitcast.4, bf16[2,16,1024]{2,1,0:T(8,128)(2,1)S(1)} %get-tuple-element.13.gate_ref, bf16[2,16,1024]{2,1,0:T(8,128)(2,1)S(1)} %collective-permute-done.1.other_ref, bf16[2,512,1024]{2,1,0:T(8,128)(2,1)S(1)} %copy-done), custom_call_target="tpu_custom_call" | custom-call | tf_op jit(solution)/shard_map/inverse_blocks/pallas_call | solution.py:282
Async XLA Ops:
  0.0 3.8 %collective-permute-start = (bf16[3,64,1024]{2,1,0:T(8,128)(2,1)}, bf16[3,64,1024]{2,1,0:T(8,128)(2,1)S(1)}, u32[]{:S(2)}, u32[]{:S(2)}) collective-permute-start(bf16[3,64,1024]{2,1,0:T(8,128)(2,1)} %own_ref.1), channel_id=1, source_target_pairs={{0,1},{1,0},{2,3},{3,2},{4,5},{5,4},{6,7},{7,6},{8,9},{9,8},{10,11... | collective-permute-start | bytes 1179656 | tf_op jit(solution)/shard_map/ppermute | solution.py:297
  1.9 1.9 %copy-start = (bf16[2,512,1024]{2,1,0:T(8,128)(2,1)S(1)}, bf16[2,512,1024]{2,1,0:T(8,128)(2,1)}, u32[]{:S(2)}) copy-start(bf16[2,512,1024]{2,1,0:T(8,128)(2,1)} %constant.2.clone.wave) | copy-start | bytes 6291460
  1.9 1.9 %copy-start.1 = (bf16[3,64,1024]{2,1,0:T(8,128)(2,1)S(1)}, bf16[3,64,1024]{2,1,0:T(8,128)(2,1)}, u32[]{:S(2)}) copy-start(bf16[3,64,1024]{2,1,0:T(8,128)(2,1)} %own_ref.1) | copy-start | bytes 1179652
  1.9 1.9 %copy-start.2 = (f32[1,4096]{1,0:T(1,128)S(1)}, f32[1,4096]{1,0:T(1,128)}, u32[]{:S(2)}) copy-start(f32[1,4096]{1,0:T(1,128)} %taps_ref.1) | copy-start | bytes 49156
  1.9 1.9 %copy-start.3 = (s32[32]{0:T(128)S(1)}, s32[32]{0:T(128)}, u32[]{:S(2)}) copy-start(s32[32]{0:T(128)} %live_ref.1) | copy-start | bytes 388
  3.4 42.8 %copy-start.4 = (f32[1,128]{1,0:T(1,128)S(1)}, f32[1,128]{1,0:T(1,128)}, u32[]{:S(2)}) copy-start(f32[1,128]{1,0:T(1,128)} %lane_gains.1.gain_ref) | copy-start | bytes 1540
  49.5 19.9 %all-to-all-start.1 = ((bf16[128,8,128]{2,1,0:T(8,128)(2,1)}), bf16[128,8,128]{2,1,0:T(8,128)(2,1)S(1)}, u32[]{:S(2)}, u32[]{:S(2)}) async-start(bf16[128,8,128]{2,1,0:T(8,128)(2,1)} %mix_blocks.1), calls=%async_computation.1 | async-start | bytes 524288 | tf_op jit(solution)/shard_map/all_to_all | solution.py:303
  56.3 10.7 %collective-permute-start.1 = (bf16[2,16,1024]{2,1,0:T(8,128)(2,1)S(1)}, bf16[2,16,1024]{2,1,0:T(8,128)(2,1)S(1)}, u32[]{:S(2)}, u32[]{:S(2)}) collective-permute-start(bf16[2,16,1024]{2,1,0:T(8,128)(2,1)S(1)} %get-tuple-element.14), channel_id=1, source_target_pairs={{0,2},{2,0},{1,3},{3,1},{4,6},{6,4},{5,7},{7,5},{8,10},{10,8},{9,1... | collective-permute-start | bytes 196616 | tf_op jit(solution)/shard_map/ppermute | solution.py:300

commit v3 on v2

--- a/solution.py
+++ b/solution.py
@@ -44,10 +44,8 @@
 
 
 def swap_parts(v):
-    is_real = (lane_ids(v.shape) // GROUP) % 2 == 0
-    up = pltpu.roll(v, LANES - GROUP, 1)
-    down = pltpu.roll(v, GROUP, 1)
-    return jnp.where(is_real, -up, down)
+    turned = pltpu.roll(v, HALF, 1)
+    return jnp.where(lane_ids(v.shape) < HALF, -turned, turned)
 
 
 def gain_kernel(gain_ref, out_ref):
@@ -70,7 +68,7 @@
     live_ref, own_ref, got_ref, taps_ref, wave, out_ref, gate_ref, send_ref, cols, packed
 ):
     high, core = lax.axis_index("yh"), lax.axis_index("core")
-    count = 4 * GROUP
+    side = 2 * GROUP
     piece = (GROUP, LANES)
     even = lane_ids(piece) % 2 == 0
     for part in range(2):
@@ -80,16 +78,15 @@
             def read(i, at):
                 return jnp.where(core == blk, own_ref[i, rows, at], got_ref[i, rows, at])
 
-            to = (2 * part + blk) * GROUP
+            to = part * HALF + blk * GROUP
             for block in range(BLOCK // LANES):
                 at = pl.ds(block * LANES, LANES)
                 live = live_ref[(2 * high + blk) * (BLOCK // LANES) + block].astype(jnp.float32)
                 key, value = read(1, at).astype(jnp.float32), read(2, at).astype(jnp.float32)
                 value = key * value * live
-                cols[pl.ds(to, GROUP), at] = jnp.where(even, value, 0.0).astype(jnp.bfloat16)
-                cols[pl.ds(count + to, GROUP), at] = jnp.where(even, 0.0, value).astype(
-                    jnp.bfloat16
-                )
+                cols[pl.ds(to, GROUP), at] = value.astype(jnp.bfloat16)
+                value = jnp.where(even, value, -value)
+                cols[pl.ds(to + side, GROUP), at] = value.astype(jnp.bfloat16)
             gate = read(0, slice(None))
 
             @pl.when(high == part)
@@ -106,8 +103,8 @@
     )
     top = taps.astype(jnp.bfloat16).astype(jnp.float32)
     taps = jnp.concatenate([top, taps - top, top, taps - top], axis=0)
-    kept = even == (row_ids((GROUP, BLOCK)) < 2 * CHAN)
-    cols[pl.ds(LANES, GROUP), :] = jnp.where(kept, taps, 0.0).astype(jnp.bfloat16)
+    plain = even | (row_ids((GROUP, BLOCK)) < 2 * CHAN)
+    cols[pl.ds(LANES, GROUP), :] = jnp.where(plain, taps, -taps).astype(jnp.bfloat16)
     cols[pl.ds(LANES + GROUP, LANES - GROUP), :] = jnp.zeros(
         (LANES - GROUP, BLOCK), jnp.bfloat16
     )
@@ -129,25 +126,14 @@
     for i in range(QUAD):
         at = slice(i * SEQ, (i + 1) * SEQ)
         cos, sin = sums[0][at, :LANES], sums[1][at, :LANES]
-        turn_cos, turn_sin = pltpu.roll(cos, HALF, 1), pltpu.roll(sin, HALF, 1)
-        real = jnp.where(lane < HALF, cos + turn_cos, turn_cos - cos)
-        imag = jnp.where(lane < HALF, sin + turn_sin, sin - turn_sin)
-        place = (lane % HALF) // GROUP
-        middle = pltpu.roll(jnp.where(place == 0, imag, real), GROUP, 1)
-        last = pltpu.roll(imag, 2 * GROUP, 1)
-        put(i, jnp.where(place == 0, real, jnp.where(place == 3, last, middle)))
-        middle = pltpu.roll(jnp.where(place == 2, imag, real), LANES - GROUP, 1)
-        last = pltpu.roll(real, LANES - 2 * GROUP, 1)
-        put(MESSAGE + i, jnp.where(place == 3, imag, jnp.where(place == 0, last, middle)))
+        sin = jnp.where(lane % HALF < side, sin, -sin)
+        put(i, jnp.where(lane < HALF, cos, pltpu.roll(sin, HALF, 1)))
+        put(MESSAGE + i, jnp.where(lane < HALF, pltpu.roll(cos, HALF, 1), sin))
         for part in range(2):
             move = part * HALF + i * GROUP
             value = sums[part][at, LANES:]
             comb = comb + (pltpu.roll(value, move, 1) if move else value)
-    step = 2 * CHAN
-    difference = pltpu.roll(comb, step, 1) - comb
-    difference = jnp.where(lane < HALF, difference, -difference)
-    both = comb + pltpu.roll(comb, LANES - step, 1)
-    comb = jnp.where((lane // step) % 2 == 0, both, difference)
+    comb = jnp.where((lane >= HALF) & ((lane // (2 * CHAN)) % 2 == 1), -comb, comb)
     comb = comb + pltpu.roll(comb, LANES - CHAN, 1)
     top = comb.astype(jnp.bfloat16).astype(jnp.float32)
     comb = jnp.where((lane // CHAN) % 2 == 0, top, pltpu.roll(comb - top, CHAN, 1))
@@ -197,7 +183,25 @@
     spec = (turned[:HALF] - before[HALF:], turned[HALF:] + before[:HALF])
     causal = lane <= row
     gain = gain_ref[...]
-    is_real = (lane // GROUP) % 2 == 0
+    low_lane = lane % HALF < 2 * GROUP
+    signals, rows = [], []
+    for k in range(FREQ):
+        digit, mirror = k // 2, k % 2
+        low, high = take(digit), take(MESSAGE + digit)
+        if mirror == 0:
+            signal = jnp.where(low_lane, low, pltpu.roll(high, 2 * GROUP, 1))
+        else:
+            signal = jnp.where(low_lane, pltpu.roll(low, LANES - 2 * GROUP, 1), high)
+        late = jnp.where(row == 0, 0.0, pltpu.roll(signal, 1, 0))
+        signals.append(signal)
+        rows.append(jnp.concatenate([signal, late], axis=1).astype(jnp.bfloat16))
+    rows = jnp.concatenate(rows, axis=0)
+    shape = (2 * LANES, (CHAN - 1) * LANES)
+    source, target = row_ids(shape), lane_ids(shape)
+    place = source % HALF + GROUP * (target // LANES + 1) - jnp.where(source < LANES, 0, HALF)
+    same_part = (source // HALF) % 2 == (target // HALF) % 2
+    shifts = jnp.where(same_part & (place == target % HALF), 1.0, 0.0).astype(jnp.bfloat16)
+    moved = jnp.dot(rows, shifts, preferred_element_type=jnp.float32).astype(jnp.bfloat16)
     for k in range(FREQ):
         digit, mirror = k // 2, k % 2
         base = digit * 4 * CHAN + mirror * 2 * CHAN
@@ -208,17 +212,10 @@
                 toeplitz = pltpu.roll(tall, 0, 1, stride=1, stride_axis=0)
                 toeplitz = jnp.where(causal, toeplitz, 0.0)
                 matrix[pl.ds(part * SEQ, SEQ), pl.ds(q * SEQ, SEQ)] = toeplitz.astype(jnp.bfloat16)
-        low, high = take(digit), take(MESSAGE + digit)
-        if mirror == 0:
-            signal = jnp.where(lane < HALF, low, pltpu.roll(high, HALF, 1))
-        else:
-            signal = jnp.where(lane < HALF, pltpu.roll(low, HALF, 1), high)
-        late = jnp.where(row == 0, 0.0, pltpu.roll(signal, 1, 0))
-        shifted = [signal.astype(jnp.bfloat16)]
-        for q in range(1, CHAN):
-            move = 2 * GROUP * q
-            moved = jnp.where(lane >= LANES - move, late, signal)
-            shifted.append(pltpu.roll(moved, move, 1).astype(jnp.bfloat16))
+        signal = signals[k]
+        at = slice(k * SEQ, (k + 1) * SEQ)
+        shifted = [rows[at, :LANES]]
+        shifted += [moved[at, q * LANES : (q + 1) * LANES] for q in range(CHAN - 1)]
         parts = jnp.dot(
             matrix[...], jnp.concatenate(shifted, axis=0), preferred_element_type=jnp.float32
         )
@@ -227,8 +224,8 @@
             first = mixed
             continue
         plus, minus = first + mixed, first - mixed
-        wide[:, digit, :] = jnp.where(is_real, plus, minus)
-        wide[:, QUAD + digit, :] = jnp.where(is_real, minus, plus)
+        wide[:, digit, :] = jnp.where(lane < HALF, plus, minus)
+        wide[:, QUAD + digit, :] = jnp.where(lane < HALF, minus, plus)
     out_ref[...] = wide[...].astype(jnp.bfloat16)
 
 
@@ -258,11 +255,7 @@
     sides = [jnp.concatenate(side, axis=1).astype(jnp.bfloat16) for side in sides]
     total = None
     for part in range(2):
-        lines = [
-            side[(2 * p + part) * GROUP : (2 * p + part + 1) * GROUP, :]
-            for side in sides
-            for p in range(CHAN)
-        ]
+        lines = [side[part * HALF : (part + 1) * HALF, :] for side in sides]
         term = jnp.dot(
             jnp.concatenate(lines, axis=0), wave[part], preferred_element_type=jnp.float32
         )

time: 70.9 us -> 69.7 us (0.983)
  Pallas kernels: 7.94 us -> 6.75 us
    pallas_call x1, Pallas kernels: 3.3 us -> 2.4 us  [mix_blocks(): pl.pallas_call(mix_kernel, out_shape=jax.ShapeDtypeStruct((SEQ, FREQ, LAN...]
where the time goes in v3:
time: 69.7 us; the launch traced here: 69.4 us
  blocking collectives  40.3 us (58%)
  starting transfers between devices  13.1 us (19%)
  waiting for transfers between devices  9.18 us (13%)
  Pallas kernels  6.75 us (10%)
    all_to_all x1, blocking collectives, body(): exchange(sent.reshape(-1, 2, LANES), ('seq', 'yh')).reshape(-1, LANES)  40.3 us
    all_to_all x1, starting transfers between devices, body(): spec = exchange(mixed, 'seq').reshape(BLOCK, LANES)  6.79 us
    ppermute x1, waiting for transfers between devices, body(): other = lax.ppermute(send, 'yh', swap)  6.29 us
    ppermute x1, starting transfers between devices, body(): other = lax.ppermute(send, 'yh', swap)  4.38 us
    all_to_all x1, waiting for transfers between devices, body(): spec = exchange(mixed, 'seq').reshape(BLOCK, LANES)  2.42 us
    pallas_call x1, Pallas kernels, mix_blocks(): pl.pallas_call(mix_kernel, out_shape=jax.ShapeDtypeStruct((SEQ, FREQ, LAN...  2.4 us
    ppermute x1, starting transfers between devices, body(): got = lax.ppermute(projected, 'core', swap)  1.91 us
    pallas_call x1, Pallas kernels, forward_blocks(): pl.pallas_call(forward_kernel, out_shape=[jax.ShapeDtypeStruct((SEQ * PAI...  1.75 us
  transfers between devices with their start and end apart: 3, of which 3 were waited for; matrix products, arithmetic and copies ran while one was open for 0% of the time, Pallas kernels for 2%

profile of v3, /device:TPU:2, one launch (start us, length us, event | category | flops | bytes accessed | tf_op | source)
XLA Modules:
  0.0 69.4 jit_solution(2431653845296815692)
XLA Ops:
  0.0 1.9 %collective-permute-start = (bf16[3,64,1024]{2,1,0:T(8,128)(2,1)}, bf16[3,64,1024]{2,1,0:T(8,128)(2,1)S(1)}, u32[]{:S(2)}, u32[]{:S(2)}) collective-permute-start(bf16[3,64,1024]{2,1,0:T(8,128)(2,1)} %own_ref.1), channel_id=1, source_target_pairs={{0,1},{1,0},{2,3},{3,2},{4,5},{5,4},{6,7},{7,6},{8,9},{9,8},{10,11... | collective-permute-start | bytes 1179656 | tf_op jit(solution)/shard_map/ppermute | solution.py:290
  1.9 0.0 copy-start
  1.9 0.0 copy-start.1
  1.9 0.0 copy-start.2
  1.9 0.0 copy-start.3
  2.0 1.4 %lane_gains.1.gain_ref = f32[1,128]{1,0:T(1,128)} custom-call(f32[1,16]{1,0:T(1,128)} %bitcast.7), custom_call_target="tpu_custom_call" | custom-call | flops 6000000000 | bytes 20000000 | tf_op jit(solution)/shard_map/lane_gains/pallas_call | solution.py:56
  3.4 0.0 copy-start.4
  3.4 0.5 collective-permute-done.got_ref
  3.8 0.0 copy-done
  3.8 0.0 copy-done.1
  3.8 0.0 copy-done.2
  3.8 0.0 copy-done.3
  3.8 1.8 %forward_blocks.1 = (bf16[1536,128]{1,0:T(8,128)(2,1)S(1)}, bf16[2,16,1024]{2,1,0:T(8,128)(2,1)S(1)}, bf16[2,16,1024]{2,1,0:T(8,128)(2,1)S(1)}) custom-call(s32[32]{0:T(128)S(1)} %copy-done.3, bf16[3,64,1024]{2,1,0:T(8,128)(2,1)S(1)} %copy-done.1, bf16[3,64,1024]{2,1,0:T(8,128)(2,1)S(1)} %collective-permute-done.got_ref, f32[1,4096]{1,0:T(1,128)S(1)} %copy-done.2, ...), custom_call_target="tpu_custom_call" | custom-call | tf_op jit(solution)/shard_map/forward_blocks/pallas_call | solution.py:150
  5.6 40.3 %all_to_all.10 = bf16[768,2,128]{2,1,0:T(2,128)(2,1)S(1)} all-to-all(bf16[768,2,128]{2,1,0:T(2,128)(2,1)S(1)} %bitcast.5), channel_id=1, replica_groups=mesh['seq'=128,'yh'=2,'core'=2] {'seq','yh'}, dimensions={0} | all-to-all | bytes 786432 | tf_op jit(solution)/shard_map/all_to_all | solution.py:294
  45.9 0.0 copy-done.4
  45.9 2.4 %mix_blocks.1 = bf16[128,8,128]{2,1,0:T(8,128)(2,1)} custom-call(bf16[1536,128]{1,0:T(8,128)(2,1)S(1)} %bitcast.6, f32[1,128]{1,0:T(1,128)S(1)} %copy-done.4), custom_call_target="tpu_custom_call" | custom-call | flops 6000000000 | bytes 20000000 | tf_op jit(solution)/shard_map/mix_blocks/pallas_call | solution.py:233
  48.3 6.8 %all-to-all-start.1 = ((bf16[128,8,128]{2,1,0:T(8,128)(2,1)}), bf16[128,8,128]{2,1,0:T(8,128)(2,1)S(1)}, u32[]{:S(2)}, u32[]{:S(2)}) async-start(bf16[128,8,128]{2,1,0:T(8,128)(2,1)} %mix_blocks.1), calls=%async_computation.1 | async-start | bytes 524288 | tf_op jit(solution)/shard_map/all_to_all | solution.py:296
  55.1 4.4 %collective-permute-start.1 = (bf16[2,16,1024]{2,1,0:T(8,128)(2,1)S(1)}, bf16[2,16,1024]{2,1,0:T(8,128)(2,1)S(1)}, u32[]{:S(2)}, u32[]{:S(2)}) collective-permute-start(bf16[2,16,1024]{2,1,0:T(8,128)(2,1)S(1)} %get-tuple-element.14), channel_id=1, source_target_pairs={{0,2},{2,0},{1,3},{3,1},{4,6},{6,4},{5,7},{7,5},{8,10},{10,8},{9,1... | collective-permute-start | bytes 196616 | tf_op jit(solution)/shard_map/ppermute | solution.py:293
  59.5 6.3 %collective-permute-done.1.other_ref = bf16[2,16,1024]{2,1,0:T(8,128)(2,1)S(1)} collective-permute-done((bf16[2,16,1024]{2,1,0:T(8,128)(2,1)S(1)}, bf16[2,16,1024]{2,1,0:T(8,128)(2,1)S(1)}, u32[]{:S(2)}, u32[]{:S(2)}) %collective-permute-start.1) | collective-permute-done | bytes 65568 | tf_op jit(solution)/shard_map/ppermute | solution.py:293
  65.8 2.4 %all-to-all-done.1 = bf16[128,8,128]{2,1,0:T(8,128)(2,1)S(1)} async-done(((bf16[128,8,128]{2,1,0:T(8,128)(2,1)}), bf16[128,8,128]{2,1,0:T(8,128)(2,1)S(1)}, u32[]{:S(2)}, u32[]{:S(2)}) %all-to-all-start.1) | async-done | bytes 262176 | tf_op jit(solution)/shard_map/all_to_all | solution.py:296
  68.2 1.2 %inverse_blocks.1 = bf16[16,4096]{1,0:T(8,128)(2,1)} custom-call(bf16[1024,128]{1,0:T(8,128)(2,1)S(1)} %bitcast.4, bf16[2,16,1024]{2,1,0:T(8,128)(2,1)S(1)} %get-tuple-element.13.gate_ref, bf16[2,16,1024]{2,1,0:T(8,128)(2,1)S(1)} %collective-permute-done.1.other_ref, bf16[2,512,1024]{2,1,0:T(8,128)(2,1)S(1)} %copy-done), custom_call_target="tpu_custom_call" | custom-call | tf_op jit(solution)/shard_map/inverse_blocks/pallas_call | solution.py:275
Async XLA Ops:
  0.0 3.8 %collective-permute-start = (bf16[3,64,1024]{2,1,0:T(8,128)(2,1)}, bf16[3,64,1024]{2,1,0:T(8,128)(2,1)S(1)}, u32[]{:S(2)}, u32[]{:S(2)}) collective-permute-start(bf16[3,64,1024]{2,1,0:T(8,128)(2,1)} %own_ref.1), channel_id=1, source_target_pairs={{0,1},{1,0},{2,3},{3,2},{4,5},{5,4},{6,7},{7,6},{8,9},{9,8},{10,11... | collective-permute-start | bytes 1179656 | tf_op jit(solution)/shard_map/ppermute | solution.py:290
  1.9 1.9 %copy-start = (bf16[2,512,1024]{2,1,0:T(8,128)(2,1)S(1)}, bf16[2,512,1024]{2,1,0:T(8,128)(2,1)}, u32[]{:S(2)}) copy-start(bf16[2,512,1024]{2,1,0:T(8,128)(2,1)} %constant.2.clone.wave) | copy-start | bytes 6291460
  1.9 1.9 %copy-start.1 = (bf16[3,64,1024]{2,1,0:T(8,128)(2,1)S(1)}, bf16[3,64,1024]{2,1,0:T(8,128)(2,1)}, u32[]{:S(2)}) copy-start(bf16[3,64,1024]{2,1,0:T(8,128)(2,1)} %own_ref.1) | copy-start | bytes 1179652
  1.9 1.9 %copy-start.2 = (f32[1,4096]{1,0:T(1,128)S(1)}, f32[1,4096]{1,0:T(1,128)}, u32[]{:S(2)}) copy-start(f32[1,4096]{1,0:T(1,128)} %taps_ref.1) | copy-start | bytes 49156
  1.9 1.9 %copy-start.3 = (s32[32]{0:T(128)S(1)}, s32[32]{0:T(128)}, u32[]{:S(2)}) copy-start(s32[32]{0:T(128)} %live_ref.1) | copy-start | bytes 388
  3.4 42.5 %copy-start.4 = (f32[1,128]{1,0:T(1,128)S(1)}, f32[1,128]{1,0:T(1,128)}, u32[]{:S(2)}) copy-start(f32[1,128]{1,0:T(1,128)} %lane_gains.1.gain_ref) | copy-start | bytes 1540
  48.3 19.9 %all-to-all-start.1 = ((bf16[128,8,128]{2,1,0:T(8,128)(2,1)}), bf16[128,8,128]{2,1,0:T(8,128)(2,1)S(1)}, u32[]{:S(2)}, u32[]{:S(2)}) async-start(bf16[128,8,128]{2,1,0:T(8,128)(2,1)} %mix_blocks.1), calls=%async_computation.1 | async-start | bytes 524288 | tf_op jit(solution)/shard_map/all_to_all | solution.py:296
  55.1 10.7 %collective-permute-start.1 = (bf16[2,16,1024]{2,1,0:T(8,128)(2,1)S(1)}, bf16[2,16,1024]{2,1,0:T(8,128)(2,1)S(1)}, u32[]{:S(2)}, u32[]{:S(2)}) collective-permute-start(bf16[2,16,1024]{2,1,0:T(8,128)(2,1)S(1)} %get-tuple-element.14), channel_id=1, source_target_pairs={{0,2},{2,0},{1,3},{3,1},{4,6},{6,4},{5,7},{7,5},{8,10},{10,8},{9,1... | collective-permute-start | bytes 196616 | tf_op jit(solution)/shard_map/ppermute | solution.py:293

commit v4 on v3

--- a/solution.py
+++ b/solution.py
@@ -142,7 +142,7 @@
     empty = jnp.zeros(square, jnp.float32)
     put(SIGNAL + 1, empty)
     put(MESSAGE + SIGNAL + 1, empty)
-    out_ref[...] = packed[...].astype(jnp.bfloat16)
+    out_ref[...] = packed[pl.ds(0, SEQ * PAIR), :].astype(jnp.bfloat16)
 
 
 def forward_blocks(live_blocks, own, got, taps, wave):
@@ -154,7 +154,7 @@
         out_specs=[ON_CHIP] * 3,
         scratch_shapes=[
             pltpu.VMEM((2 * LANES, BLOCK), jnp.bfloat16),
-            pltpu.VMEM((SEQ * PAIR, LANES), jnp.float32),
+            pltpu.VMEM(((SEQ + 1) * PAIR, LANES), jnp.float32),
         ],
         compiler_params=pltpu.CompilerParams(vmem_limit_bytes=48 * MIB),
         name="forward_blocks",
@@ -162,7 +162,7 @@
 
 
 def mix_kernel(in_ref, gain_ref, out_ref, spread, wide, matrix):
-    spread[...] = in_ref[...].astype(jnp.float32)
+    spread[pl.ds(0, SEQ * PAIR), :] = in_ref[...].astype(jnp.float32)
     square = (SEQ, LANES)
     row, lane = row_ids(square), lane_ids(square)
 
@@ -236,7 +236,7 @@
         in_specs=[ON_CHIP, ON_CHIP],
         out_specs=ON_CHIP,
         scratch_shapes=[
-            pltpu.VMEM((SEQ * PAIR, LANES), jnp.float32),
+            pltpu.VMEM(((SEQ + 1) * PAIR, LANES), jnp.float32),
             pltpu.VMEM((SEQ, FREQ, LANES), jnp.float32),
             pltpu.VMEM((2 * SEQ, CHAN * SEQ), jnp.bfloat16),
         ],
@@ -247,7 +247,7 @@
 
 
 def inverse_kernel(spec_ref, gate_ref, other_ref, wave, out_ref, plain):
-    plain[...] = spec_ref[...].astype(jnp.float32)
+    plain[pl.ds(0, BLOCK), :] = spec_ref[...].astype(jnp.float32)
     sides = [
         [plain[pl.ds(part * QUAD + i, SEQ, stride=FREQ), :].T for i in range(QUAD)]
         for part in range(2)
@@ -277,7 +277,7 @@
         out_shape=jax.ShapeDtypeStruct((GROUP, CHAN * BLOCK), jnp.bfloat16),
         in_specs=[ON_CHIP] * 4,
         out_specs=ON_CHIP,
-        scratch_shapes=[pltpu.VMEM((BLOCK, LANES), jnp.float32)],
+        scratch_shapes=[pltpu.VMEM((BLOCK + FREQ, LANES), jnp.float32)],
         compiler_params=pltpu.CompilerParams(vmem_limit_bytes=48 * MIB),
         name="inverse_blocks",
     )(spec, gate, other, wave)

time: 69.7 us -> 69.7 us (level)
  no operation moved by 1% of the time
where the time goes in v4:
time: 69.7 us; the launch traced here: 69.4 us
  blocking collectives  40.3 us (58%)
  starting transfers between devices  13.1 us (19%)
  waiting for transfers between devices  9.18 us (13%)
  Pallas kernels  6.75 us (10%)
    all_to_all x1, blocking collectives, body(): exchange(sent.reshape(-1, 2, LANES), ('seq', 'yh')).reshape(-1, LANES)  40.3 us
    all_to_all x1, starting transfers between devices, body(): spec = exchange(mixed, 'seq').reshape(BLOCK, LANES)  6.79 us
    ppermute x1, waiting for transfers between devices, body(): other = lax.ppermute(send, 'yh', swap)  6.29 us
    ppermute x1, starting transfers between devices, body(): other = lax.ppermute(send, 'yh', swap)  4.38 us
    all_to_all x1, waiting for transfers between devices, body(): spec = exchange(mixed, 'seq').reshape(BLOCK, LANES)  2.42 us
    pallas_call x1, Pallas kernels, mix_blocks(): pl.pallas_call(mix_kernel, out_shape=jax.ShapeDtypeStruct((SEQ, FREQ, LAN...  2.4 us
    ppermute x1, starting transfers between devices, body(): got = lax.ppermute(projected, 'core', swap)  1.91 us
    pallas_call x1, Pallas kernels, forward_blocks(): pl.pallas_call(forward_kernel, out_shape=[jax.ShapeDtypeStruct((SEQ * PAI...  1.75 us
  transfers between devices with their start and end apart: 3, of which 3 were waited for; matrix products, arithmetic and copies ran while one was open for 0% of the time, Pallas kernels for 2%

profile of v4, /device:TPU:2, one launch (start us, length us, event | category | flops | bytes accessed | tf_op | source)
XLA Modules:
  0.0 69.4 jit_solution(14412970172079321227)
XLA Ops:
  0.0 1.9 %collective-permute-start = (bf16[3,64,1024]{2,1,0:T(8,128)(2,1)}, bf16[3,64,1024]{2,1,0:T(8,128)(2,1)S(1)}, u32[]{:S(2)}, u32[]{:S(2)}) collective-permute-start(bf16[3,64,1024]{2,1,0:T(8,128)(2,1)} %own_ref.1), channel_id=1, source_target_pairs={{0,1},{1,0},{2,3},{3,2},{4,5},{5,4},{6,7},{7,6},{8,9},{9,8},{10,11... | collective-permute-start | bytes 1179656 | tf_op jit(solution)/shard_map/ppermute | solution.py:290
  1.9 0.0 copy-start
  1.9 0.0 copy-start.1
  1.9 0.0 copy-start.2
  1.9 0.0 copy-start.3
  2.0 1.4 %lane_gains.1.gain_ref = f32[1,128]{1,0:T(1,128)} custom-call(f32[1,16]{1,0:T(1,128)} %bitcast.7), custom_call_target="tpu_custom_call" | custom-call | flops 6000000000 | bytes 20000000 | tf_op jit(solution)/shard_map/lane_gains/pallas_call | solution.py:56
  3.4 0.0 copy-start.4
  3.4 0.5 collective-permute-done.got_ref
  3.8 0.0 copy-done
  3.8 0.0 copy-done.1
  3.8 0.0 copy-done.2
  3.8 0.0 copy-done.3
  3.8 1.8 %forward_blocks.1 = (bf16[1536,128]{1,0:T(8,128)(2,1)S(1)}, bf16[2,16,1024]{2,1,0:T(8,128)(2,1)S(1)}, bf16[2,16,1024]{2,1,0:T(8,128)(2,1)S(1)}) custom-call(s32[32]{0:T(128)S(1)} %copy-done.3, bf16[3,64,1024]{2,1,0:T(8,128)(2,1)S(1)} %copy-done.1, bf16[3,64,1024]{2,1,0:T(8,128)(2,1)S(1)} %collective-permute-done.got_ref, f32[1,4096]{1,0:T(1,128)S(1)} %copy-done.2, ...), custom_call_target="tpu_custom_call" | custom-call | tf_op jit(solution)/shard_map/forward_blocks/pallas_call | solution.py:150
  5.6 40.3 %all_to_all.10 = bf16[768,2,128]{2,1,0:T(2,128)(2,1)S(1)} all-to-all(bf16[768,2,128]{2,1,0:T(2,128)(2,1)S(1)} %bitcast.5), channel_id=1, replica_groups=mesh['seq'=128,'yh'=2,'core'=2] {'seq','yh'}, dimensions={0} | all-to-all | bytes 786432 | tf_op jit(solution)/shard_map/all_to_all | solution.py:294
  45.9 0.0 copy-done.4
  45.9 2.4 %mix_blocks.1 = bf16[128,8,128]{2,1,0:T(8,128)(2,1)} custom-call(bf16[1536,128]{1,0:T(8,128)(2,1)S(1)} %bitcast.6, f32[1,128]{1,0:T(1,128)S(1)} %copy-done.4), custom_call_target="tpu_custom_call" | custom-call | flops 6000000000 | bytes 20000000 | tf_op jit(solution)/shard_map/mix_blocks/pallas_call | solution.py:233
  48.3 6.8 %all-to-all-start.1 = ((bf16[128,8,128]{2,1,0:T(8,128)(2,1)}), bf16[128,8,128]{2,1,0:T(8,128)(2,1)S(1)}, u32[]{:S(2)}, u32[]{:S(2)}) async-start(bf16[128,8,128]{2,1,0:T(8,128)(2,1)} %mix_blocks.1), calls=%async_computation.1 | async-start | bytes 524288 | tf_op jit(solution)/shard_map/all_to_all | solution.py:296
  55.1 4.4 %collective-permute-start.1 = (bf16[2,16,1024]{2,1,0:T(8,128)(2,1)S(1)}, bf16[2,16,1024]{2,1,0:T(8,128)(2,1)S(1)}, u32[]{:S(2)}, u32[]{:S(2)}) collective-permute-start(bf16[2,16,1024]{2,1,0:T(8,128)(2,1)S(1)} %get-tuple-element.14), channel_id=1, source_target_pairs={{0,2},{2,0},{1,3},{3,1},{4,6},{6,4},{5,7},{7,5},{8,10},{10,8},{9,1... | collective-permute-start | bytes 196616 | tf_op jit(solution)/shard_map/ppermute | solution.py:293
  59.5 6.3 %collective-permute-done.1.other_ref = bf16[2,16,1024]{2,1,0:T(8,128)(2,1)S(1)} collective-permute-done((bf16[2,16,1024]{2,1,0:T(8,128)(2,1)S(1)}, bf16[2,16,1024]{2,1,0:T(8,128)(2,1)S(1)}, u32[]{:S(2)}, u32[]{:S(2)}) %collective-permute-start.1) | collective-permute-done | bytes 65568 | tf_op jit(solution)/shard_map/ppermute | solution.py:293
  65.8 2.4 %all-to-all-done.1 = bf16[128,8,128]{2,1,0:T(8,128)(2,1)S(1)} async-done(((bf16[128,8,128]{2,1,0:T(8,128)(2,1)}), bf16[128,8,128]{2,1,0:T(8,128)(2,1)S(1)}, u32[]{:S(2)}, u32[]{:S(2)}) %all-to-all-start.1) | async-done | bytes 262176 | tf_op jit(solution)/shard_map/all_to_all | solution.py:296
  68.2 1.2 %inverse_blocks.1 = bf16[16,4096]{1,0:T(8,128)(2,1)} custom-call(bf16[1024,128]{1,0:T(8,128)(2,1)S(1)} %bitcast.4, bf16[2,16,1024]{2,1,0:T(8,128)(2,1)S(1)} %get-tuple-element.13.gate_ref, bf16[2,16,1024]{2,1,0:T(8,128)(2,1)S(1)} %collective-permute-done.1.other_ref, bf16[2,512,1024]{2,1,0:T(8,128)(2,1)S(1)} %copy-done), custom_call_target="tpu_custom_call" | custom-call | tf_op jit(solution)/shard_map/inverse_blocks/pallas_call | solution.py:275
Async XLA Ops:
  0.0 3.8 %collective-permute-start = (bf16[3,64,1024]{2,1,0:T(8,128)(2,1)}, bf16[3,64,1024]{2,1,0:T(8,128)(2,1)S(1)}, u32[]{:S(2)}, u32[]{:S(2)}) collective-permute-start(bf16[3,64,1024]{2,1,0:T(8,128)(2,1)} %own_ref.1), channel_id=1, source_target_pairs={{0,1},{1,0},{2,3},{3,2},{4,5},{5,4},{6,7},{7,6},{8,9},{9,8},{10,11... | collective-permute-start | bytes 1179656 | tf_op jit(solution)/shard_map/ppermute | solution.py:290
  1.9 1.9 %copy-start = (bf16[2,512,1024]{2,1,0:T(8,128)(2,1)S(1)}, bf16[2,512,1024]{2,1,0:T(8,128)(2,1)}, u32[]{:S(2)}) copy-start(bf16[2,512,1024]{2,1,0:T(8,128)(2,1)} %constant.2.clone.wave) | copy-start | bytes 6291460
  1.9 1.9 %copy-start.1 = (bf16[3,64,1024]{2,1,0:T(8,128)(2,1)S(1)}, bf16[3,64,1024]{2,1,0:T(8,128)(2,1)}, u32[]{:S(2)}) copy-start(bf16[3,64,1024]{2,1,0:T(8,128)(2,1)} %own_ref.1) | copy-start | bytes 1179652
  1.9 1.9 %copy-start.2 = (f32[1,4096]{1,0:T(1,128)S(1)}, f32[1,4096]{1,0:T(1,128)}, u32[]{:S(2)}) copy-start(f32[1,4096]{1,0:T(1,128)} %taps_ref.1) | copy-start | bytes 49156
  1.9 1.9 %copy-start.3 = (s32[32]{0:T(128)S(1)}, s32[32]{0:T(128)}, u32[]{:S(2)}) copy-start(s32[32]{0:T(128)} %live_ref.1) | copy-start | bytes 388
  3.4 42.5 %copy-start.4 = (f32[1,128]{1,0:T(1,128)S(1)}, f32[1,128]{1,0:T(1,128)}, u32[]{:S(2)}) copy-start(f32[1,128]{1,0:T(1,128)} %lane_gains.1.gain_ref) | copy-start | bytes 1540
  48.3 19.9 %all-to-all-start.1 = ((bf16[128,8,128]{2,1,0:T(8,128)(2,1)}), bf16[128,8,128]{2,1,0:T(8,128)(2,1)S(1)}, u32[]{:S(2)}, u32[]{:S(2)}) async-start(bf16[128,8,128]{2,1,0:T(8,128)(2,1)} %mix_blocks.1), calls=%async_computation.1 | async-start | bytes 524288 | tf_op jit(solution)/shard_map/all_to_all | solution.py:296
  55.1 10.7 %collective-permute-start.1 = (bf16[2,16,1024]{2,1,0:T(8,128)(2,1)S(1)}, bf16[2,16,1024]{2,1,0:T(8,128)(2,1)S(1)}, u32[]{:S(2)}, u32[]{:S(2)}) collective-permute-start(bf16[2,16,1024]{2,1,0:T(8,128)(2,1)S(1)} %get-tuple-element.14), channel_id=1, source_target_pairs={{0,2},{2,0},{1,3},{3,1},{4,6},{6,4},{5,7},{7,5},{8,10},{10,8},{9,1... | collective-permute-start | bytes 196616 | tf_op jit(solution)/shard_map/ppermute | solution.py:293

commit v5 on v4

--- a/solution.py
+++ b/solution.py
@@ -19,6 +19,7 @@
 SIGNAL = 4
 MESSAGE = 6
 PAIR = 2 * MESSAGE
+ANSWER = FREQ + 2
 MIB = 1024 * 1024
 COST = pl.CostEstimate(flops=6_000_000_000, bytes_accessed=20_000_000, transcendentals=0)
 ON_CHIP = pl.BlockSpec(memory_space=pltpu.VMEM)
@@ -64,8 +65,12 @@
     )(skip_gain.reshape(1, GROUP))
 
 
+def gate_pieces(blk):
+    return [(i, i % 2, blk * QUAD + i // 2) for i in range(BLOCK // LANES)]
+
+
 def forward_kernel(
-    live_ref, own_ref, got_ref, taps_ref, wave, out_ref, gate_ref, send_ref, cols, packed
+    live_ref, own_ref, got_ref, taps_ref, wave, out_ref, gate_ref, cols, packed, parcel
 ):
     high, core = lax.axis_index("yh"), lax.axis_index("core")
     side = 2 * GROUP
@@ -95,7 +100,10 @@
 
             @pl.when(high != part)
             def _():
-                send_ref[blk] = gate
+                for piece_at, row, number in gate_pieces(blk):
+                    at = pl.ds(piece_at * LANES, LANES)
+                    value = read(0, at).astype(jnp.float32)
+                    parcel[row, pl.ds(number, GROUP, stride=FREQ), :] = value
 
     even = lane_ids((GROUP, BLOCK)) % 2 == 0
     taps = jnp.concatenate(
@@ -137,11 +145,10 @@
     comb = comb + pltpu.roll(comb, LANES - CHAN, 1)
     top = comb.astype(jnp.bfloat16).astype(jnp.float32)
     comb = jnp.where((lane // CHAN) % 2 == 0, top, pltpu.roll(comb - top, CHAN, 1))
-    put(SIGNAL, jnp.where(high == 0, comb, 0.0))
-    put(MESSAGE + SIGNAL, jnp.where(high == 1, comb, 0.0))
-    empty = jnp.zeros(square, jnp.float32)
-    put(SIGNAL + 1, empty)
-    put(MESSAGE + SIGNAL + 1, empty)
+    for group in range(2):
+        at = group * MESSAGE + SIGNAL
+        put(at, jnp.where(high == group, comb, parcel[0, pl.ds(0, SEQ), :]))
+        put(at + 1, jnp.where(high == group, 0.0, parcel[1, pl.ds(0, SEQ), :]))
     out_ref[...] = packed[pl.ds(0, SEQ * PAIR), :].astype(jnp.bfloat16)
 
 
@@ -149,12 +156,13 @@
     gate = jax.ShapeDtypeStruct((2, GROUP, BLOCK), jnp.bfloat16)
     return pl.pallas_call(
         forward_kernel,
-        out_shape=[jax.ShapeDtypeStruct((SEQ * PAIR, LANES), jnp.bfloat16), gate, gate],
+        out_shape=[jax.ShapeDtypeStruct((SEQ * PAIR, LANES), jnp.bfloat16), gate],
         in_specs=[pl.BlockSpec(memory_space=pltpu.SMEM)] + [ON_CHIP] * 4,
-        out_specs=[ON_CHIP] * 3,
+        out_specs=[ON_CHIP] * 2,
         scratch_shapes=[
             pltpu.VMEM((2 * LANES, BLOCK), jnp.bfloat16),
             pltpu.VMEM(((SEQ + 1) * PAIR, LANES), jnp.float32),
+            pltpu.VMEM((2, SEQ + FREQ, LANES), jnp.float32),
         ],
         compiler_params=pltpu.CompilerParams(vmem_limit_bytes=48 * MIB),
         name="forward_blocks",
@@ -169,7 +177,12 @@
     def take(at):
         return spread[pl.ds(at, SEQ, stride=PAIR), :]
 
-    comb = take(SIGNAL) + take(MESSAGE + SIGNAL)
+    def put(row, value):
+        wide[pl.ds(row, SEQ, stride=ANSWER), :] = value
+
+    own = lax.axis_index("yh")
+    extra = [take(at + SIGNAL) for at in (0, MESSAGE)]
+    comb = jnp.where(own == 0, extra[0], extra[1])
     negate = jnp.where((row + lane) % SEQ == 0, 1.0, 0.0).astype(jnp.bfloat16)
     turned = jnp.dot(comb.T.astype(jnp.bfloat16), negate, preferred_element_type=jnp.float32)
     turned = turned + pltpu.roll(turned, LANES - CHAN, 0)
@@ -224,20 +237,22 @@
             first = mixed
             continue
         plus, minus = first + mixed, first - mixed
-        wide[:, digit, :] = jnp.where(lane < HALF, plus, minus)
-        wide[:, QUAD + digit, :] = jnp.where(lane < HALF, minus, plus)
-    out_ref[...] = wide[...].astype(jnp.bfloat16)
+        put(digit, jnp.where(lane < HALF, plus, minus))
+        put(QUAD + digit, jnp.where(lane < HALF, minus, plus))
+    put(FREQ, jnp.where(own == 0, extra[1], extra[0]))
+    put(FREQ + 1, jnp.where(own == 0, take(PAIR - 1), take(MESSAGE - 1)))
+    out_ref[...] = wide[pl.ds(0, SEQ * ANSWER), :].astype(jnp.bfloat16)
 
 
 def mix_blocks(received, gain):
     return pl.pallas_call(
         mix_kernel,
-        out_shape=jax.ShapeDtypeStruct((SEQ, FREQ, LANES), jnp.bfloat16),
+        out_shape=jax.ShapeDtypeStruct((SEQ * ANSWER, LANES), jnp.bfloat16),
         in_specs=[ON_CHIP, ON_CHIP],
         out_specs=ON_CHIP,
         scratch_shapes=[
             pltpu.VMEM(((SEQ + 1) * PAIR, LANES), jnp.float32),
-            pltpu.VMEM((SEQ, FREQ, LANES), jnp.float32),
+            pltpu.VMEM(((SEQ + 1) * ANSWER, LANES), jnp.float32),
             pltpu.VMEM((2 * SEQ, CHAN * SEQ), jnp.bfloat16),
         ],
         compiler_params=pltpu.CompilerParams(vmem_limit_bytes=48 * MIB),
@@ -246,10 +261,10 @@
     )(received, gain)
 
 
-def inverse_kernel(spec_ref, gate_ref, other_ref, wave, out_ref, plain):
-    plain[pl.ds(0, BLOCK), :] = spec_ref[...].astype(jnp.float32)
+def inverse_kernel(spec_ref, gate_ref, wave, out_ref, plain):
+    plain[pl.ds(0, SEQ * ANSWER), :] = spec_ref[...].astype(jnp.float32)
     sides = [
-        [plain[pl.ds(part * QUAD + i, SEQ, stride=FREQ), :].T for i in range(QUAD)]
+        [plain[pl.ds(part * QUAD + i, SEQ, stride=ANSWER), :].T for i in range(QUAD)]
         for part in range(2)
     ]
     sides = [jnp.concatenate(side, axis=1).astype(jnp.bfloat16) for side in sides]
@@ -267,20 +282,25 @@
         value = jnp.where(
             even, total[at : at + GROUP, :], total[HALF + at : HALF + at + GROUP, :]
         )
-        gate = jnp.where(high == p // 2, gate_ref[p % 2], other_ref[p % 2]).astype(jnp.float32)
+        other = [
+            plain[pl.ds(number * ANSWER + FREQ + row, GROUP, stride=FREQ * ANSWER), :]
+            for _, row, number in gate_pieces(p % 2)
+        ]
+        other = jnp.concatenate(other, axis=1)
+        gate = jnp.where(high == p // 2, gate_ref[p % 2].astype(jnp.float32), other)
         out_ref[:, pl.ds(p * BLOCK, BLOCK)] = (gate * (value * (1.0 / BLOCK))).astype(jnp.bfloat16)
 
 
-def inverse_blocks(spec, gate, other, wave):
+def inverse_blocks(spec, gate, wave):
     return pl.pallas_call(
         inverse_kernel,
         out_shape=jax.ShapeDtypeStruct((GROUP, CHAN * BLOCK), jnp.bfloat16),
-        in_specs=[ON_CHIP] * 4,
+        in_specs=[ON_CHIP] * 3,
         out_specs=ON_CHIP,
-        scratch_shapes=[pltpu.VMEM((BLOCK + FREQ, LANES), jnp.float32)],
+        scratch_shapes=[pltpu.VMEM(((SEQ + FREQ) * ANSWER, LANES), jnp.float32)],
         compiler_params=pltpu.CompilerParams(vmem_limit_bytes=48 * MIB),
         name="inverse_blocks",
-    )(spec, gate, other, wave)
+    )(spec, gate, wave)
 
 
 def body(projected, live_blocks, filters, skip_gain):
@@ -289,12 +309,11 @@
     swap = ((0, 1), (1, 0))
     got = lax.ppermute(projected, "core", swap)
     got, gain = lax.optimization_barrier((got, lane_gains(skip_gain)))
-    sent, gate, send = forward_blocks(live_blocks, projected, got, filters, wave)
-    other = lax.ppermute(send, "yh", swap)
+    sent, gate = forward_blocks(live_blocks, projected, got, filters, wave)
     got_spec = exchange(sent.reshape(-1, 2, LANES), ("seq", "yh")).reshape(-1, LANES)
     mixed = mix_blocks(got_spec, gain)
-    spec = exchange(mixed, "seq").reshape(BLOCK, LANES)
-    return inverse_blocks(spec, gate, other, wave)
+    spec = exchange(mixed.reshape(-1, 2, LANES), "seq").reshape(-1, LANES)
+    return inverse_blocks(spec, gate, wave)
 
 
 def solution(mesh):

time: 69.7 us -> 69.4 us (level)
  the two profiles are of different devices: /device:TPU:2 before, /device:TPU:8 now
where the time goes in v5:
time: 69.4 us; the launch traced here: 69.2 us
  blocking collectives  61 us (88%)
  Pallas kernels  5.71 us (8%)
  starting transfers between devices  1.91 us (3%)
    all_to_all x1, blocking collectives, body(): exchange(sent.reshape(-1, 2, LANES), ('seq', 'yh')).reshape(-1, LANES)  41 us
    all_to_all x1, blocking collectives, body(): spec = exchange(mixed.reshape(-1, 2, LANES), 'seq').reshape(-1, LANES)  20 us
    ppermute x1, starting transfers between devices, body(): got = lax.ppermute(projected, 'core', swap)  1.91 us
    pallas_call x1, Pallas kernels, forward_blocks(): pl.pallas_call(forward_kernel, out_shape=[jax.ShapeDtypeStruct((SEQ * PAI...  1.77 us
    pallas_call x1, Pallas kernels, lane_gains(): pl.pallas_call(gain_kernel, out_shape=jax.ShapeDtypeStruct((1, LANES), jn...  1.39 us
  transfers between devices with their start and end apart: 1, of which 1 were waited for; matrix products, arithmetic and copies ran while one was open for 0% of the time, Pallas kernels for 2%

profile of v5, /device:TPU:8, one launch (start us, length us, event | category | flops | bytes accessed | tf_op | source)
XLA Modules:
  0.0 69.2 jit_solution(15315501797507953968)
XLA Ops:
  0.0 1.9 %collective-permute-start = (bf16[3,64,1024]{2,1,0:T(8,128)(2,1)}, bf16[3,64,1024]{2,1,0:T(8,128)(2,1)S(1)}, u32[]{:S(2)}, u32[]{:S(2)}) collective-permute-start(bf16[3,64,1024]{2,1,0:T(8,128)(2,1)} %own_ref.1), channel_id=1, source_target_pairs={{0,1},{1,0},{2,3},{3,2},{4,5},{5,4},{6,7},{7,6},{8,9},{9,8},{10,11... | collective-permute-start | bytes 1179656 | tf_op jit(solution)/shard_map/ppermute | solution.py:310
  1.9 0.0 copy-start
  1.9 0.0 copy-start.1
  1.9 0.0 copy-start.2
  1.9 0.0 copy-start.3
  2.0 1.4 %lane_gains.1.gain_ref = f32[1,128]{1,0:T(1,128)} custom-call(f32[1,16]{1,0:T(1,128)} %bitcast.9), custom_call_target="tpu_custom_call" | custom-call | flops 6000000000 | bytes 20000000 | tf_op jit(solution)/shard_map/lane_gains/pallas_call | solution.py:57
  3.4 0.0 copy-start.4
  3.4 0.5 collective-permute-done.got_ref
  3.8 0.0 copy-done
  3.8 0.0 copy-done.1
  3.8 0.0 copy-done.2
  3.8 0.0 copy-done.3
  3.8 1.8 %forward_blocks.1 = (bf16[1536,128]{1,0:T(8,128)(2,1)S(1)}, bf16[2,16,1024]{2,1,0:T(8,128)(2,1)S(1)}) custom-call(s32[32]{0:T(128)S(1)} %copy-done.3, bf16[3,64,1024]{2,1,0:T(8,128)(2,1)S(1)} %copy-done.1, bf16[3,64,1024]{2,1,0:T(8,128)(2,1)S(1)} %collective-permute-done.got_ref, f32[1,4096]{1,0:T(1,128)S(1)} %copy-done.2, bf16[2,512,1024]{2,1,0:T(8,128)(2,1)S(1)} %copy-done), custom_call_target="tpu_custom_call" | custom-call | tf_op jit(solution)/shard_map/forward_blocks/pallas_call | solution.py:157
  5.6 41.0 %all_to_all.10 = bf16[768,2,128]{2,1,0:T(2,128)(2,1)S(1)} all-to-all(bf16[768,2,128]{2,1,0:T(2,128)(2,1)S(1)} %bitcast.6), channel_id=1, replica_groups=mesh['seq'=128,'yh'=2,'core'=2] {'seq','yh'}, dimensions={0} | all-to-all | bytes 786432 | tf_op jit(solution)/shard_map/all_to_all | solution.py:313
  46.6 0.0 copy-done.4
  46.6 1.3 %mix_blocks.1 = bf16[1280,128]{1,0:T(8,128)(2,1)S(1)} custom-call(bf16[1536,128]{1,0:T(8,128)(2,1)S(1)} %bitcast.7, f32[1,128]{1,0:T(1,128)S(1)} %copy-done.4), custom_call_target="tpu_custom_call" | custom-call | flops 6000000000 | bytes 20000000 | tf_op jit(solution)/shard_map/mix_blocks/pallas_call | solution.py:248
  48.0 20.0 %all_to_all.11 = bf16[640,2,128]{2,1,0:T(2,128)(2,1)S(1)} all-to-all(bf16[640,2,128]{2,1,0:T(2,128)(2,1)S(1)} %bitcast.8), channel_id=1, replica_groups=mesh['seq'=128,'yh'=2,'core'=2] {'seq'}, dimensions={0} | all-to-all | bytes 655360 | tf_op jit(solution)/shard_map/all_to_all | solution.py:315
  68.0 1.2 %inverse_blocks.1 = bf16[16,4096]{1,0:T(8,128)(2,1)} custom-call(bf16[1280,128]{1,0:T(8,128)(2,1)S(1)} %bitcast.5, bf16[2,16,1024]{2,1,0:T(8,128)(2,1)S(1)} %get-tuple-element.12.gate_ref, bf16[2,512,1024]{2,1,0:T(8,128)(2,1)S(1)} %copy-done), custom_call_target="tpu_custom_call" | custom-call | tf_op jit(solution)/shard_map/inverse_blocks/pallas_call | solution.py:295
Async XLA Ops:
  0.0 3.8 %collective-permute-start = (bf16[3,64,1024]{2,1,0:T(8,128)(2,1)}, bf16[3,64,1024]{2,1,0:T(8,128)(2,1)S(1)}, u32[]{:S(2)}, u32[]{:S(2)}) collective-permute-start(bf16[3,64,1024]{2,1,0:T(8,128)(2,1)} %own_ref.1), channel_id=1, source_target_pairs={{0,1},{1,0},{2,3},{3,2},{4,5},{5,4},{6,7},{7,6},{8,9},{9,8},{10,11... | collective-permute-start | bytes 1179656 | tf_op jit(solution)/shard_map/ppermute | solution.py:310
  1.9 1.9 %copy-start = (bf16[2,512,1024]{2,1,0:T(8,128)(2,1)S(1)}, bf16[2,512,1024]{2,1,0:T(8,128)(2,1)}, u32[]{:S(2)}) copy-start(bf16[2,512,1024]{2,1,0:T(8,128)(2,1)} %constant.2.clone.wave) | copy-start | bytes 6291460
  1.9 1.9 %copy-start.1 = (bf16[3,64,1024]{2,1,0:T(8,128)(2,1)S(1)}, bf16[3,64,1024]{2,1,0:T(8,128)(2,1)}, u32[]{:S(2)}) copy-start(bf16[3,64,1024]{2,1,0:T(8,128)(2,1)} %own_ref.1) | copy-start | bytes 1179652
  1.9 1.9 %copy-start.2 = (f32[1,4096]{1,0:T(1,128)S(1)}, f32[1,4096]{1,0:T(1,128)}, u32[]{:S(2)}) copy-start(f32[1,4096]{1,0:T(1,128)} %taps_ref.1) | copy-start | bytes 49156
  1.9 1.9 %copy-start.3 = (s32[32]{0:T(128)S(1)}, s32[32]{0:T(128)}, u32[]{:S(2)}) copy-start(s32[32]{0:T(128)} %live_ref.1) | copy-start | bytes 388
  3.4 43.3 %copy-start.4 = (f32[1,128]{1,0:T(1,128)S(1)}, f32[1,128]{1,0:T(1,128)}, u32[]{:S(2)}) copy-start(f32[1,128]{1,0:T(1,128)} %lane_gains.1.gain_ref) | copy-start | bytes 1540

commit v6 on v5

--- a/solution.py
+++ b/solution.py
@@ -73,6 +73,8 @@
     live_ref, own_ref, got_ref, taps_ref, wave, out_ref, gate_ref, cols, packed, parcel
 ):
     high, core = lax.axis_index("yh"), lax.axis_index("core")
+    lives = live_ref[...].astype(jnp.float32)
+    places = lane_ids(lives.shape)
     side = 2 * GROUP
     piece = (GROUP, LANES)
     even = lane_ids(piece) % 2 == 0
@@ -86,7 +88,8 @@
             to = part * HALF + blk * GROUP
             for block in range(BLOCK // LANES):
                 at = pl.ds(block * LANES, LANES)
-                live = live_ref[(2 * high + blk) * (BLOCK // LANES) + block].astype(jnp.float32)
+                number = (2 * high + blk) * (BLOCK // LANES) + block
+                live = jnp.sum(jnp.where(places == number, lives, 0.0), axis=1, keepdims=True)
                 key, value = read(1, at).astype(jnp.float32), read(2, at).astype(jnp.float32)
                 value = key * value * live
                 cols[pl.ds(to, GROUP), at] = value.astype(jnp.bfloat16)
@@ -157,7 +160,7 @@
     return pl.pallas_call(
         forward_kernel,
         out_shape=[jax.ShapeDtypeStruct((SEQ * PAIR, LANES), jnp.bfloat16), gate],
-        in_specs=[pl.BlockSpec(memory_space=pltpu.SMEM)] + [ON_CHIP] * 4,
+        in_specs=[ON_CHIP] * 5,
         out_specs=[ON_CHIP] * 2,
         scratch_shapes=[
             pltpu.VMEM((2 * LANES, BLOCK), jnp.bfloat16),
@@ -166,10 +169,10 @@
         ],
         compiler_params=pltpu.CompilerParams(vmem_limit_bytes=48 * MIB),
         name="forward_blocks",
-    )(live_blocks, own, got, taps, wave)
-
-
-def mix_kernel(in_ref, gain_ref, out_ref, spread, wide, matrix):
+    )(live_blocks.reshape(1, -1), own, got, taps, wave)
+
+
+def mix_kernel(in_ref, gain_ref, out_ref, spread, wide):
     spread[pl.ds(0, SEQ * PAIR), :] = in_ref[...].astype(jnp.float32)
     square = (SEQ, LANES)
     row, lane = row_ids(square), lane_ids(square)
@@ -218,19 +221,21 @@
     for k in range(FREQ):
         digit, mirror = k // 2, k % 2
         base = digit * 4 * CHAN + mirror * 2 * CHAN
+        tiles = ([], [])
         for q in range(CHAN):
             for part in range(2):
                 line = spec[part][base + q : base + q + 1, :]
                 tall = jnp.broadcast_to(line, square)
                 toeplitz = pltpu.roll(tall, 0, 1, stride=1, stride_axis=0)
                 toeplitz = jnp.where(causal, toeplitz, 0.0)
-                matrix[pl.ds(part * SEQ, SEQ), pl.ds(q * SEQ, SEQ)] = toeplitz.astype(jnp.bfloat16)
+                tiles[part].append(toeplitz.astype(jnp.bfloat16))
         signal = signals[k]
         at = slice(k * SEQ, (k + 1) * SEQ)
         shifted = [rows[at, :LANES]]
         shifted += [moved[at, q * LANES : (q + 1) * LANES] for q in range(CHAN - 1)]
+        matrix = jnp.concatenate([jnp.concatenate(line, axis=1) for line in tiles], axis=0)
         parts = jnp.dot(
-            matrix[...], jnp.concatenate(shifted, axis=0), preferred_element_type=jnp.float32
+            matrix, jnp.concatenate(shifted, axis=0), preferred_element_type=jnp.float32
         )
         mixed = parts[:SEQ, :] + swap_parts(parts[SEQ:, :]) + gain * signal
         if mirror == 0:
@@ -253,7 +258,6 @@
         scratch_shapes=[
             pltpu.VMEM(((SEQ + 1) * PAIR, LANES), jnp.float32),
             pltpu.VMEM(((SEQ + 1) * ANSWER, LANES), jnp.float32),
-            pltpu.VMEM((2 * SEQ, CHAN * SEQ), jnp.bfloat16),
         ],
         compiler_params=pltpu.CompilerParams(vmem_limit_bytes=48 * MIB),
         cost_estimate=COST,

time: 69.4 us -> 68.9 us (level)
  no operation moved by 1% of the time
where the time goes in v6:
time: 68.9 us; the launch traced here: 68.7 us
  blocking collectives  61 us (89%)
  Pallas kernels  5.22 us (8%)
  starting transfers between devices  1.91 us (3%)
    all_to_all x1, blocking collectives, body(): exchange(sent.reshape(-1, 2, LANES), ('seq', 'yh')).reshape(-1, LANES)  41 us
    all_to_all x1, blocking collectives, body(): spec = exchange(mixed.reshape(-1, 2, LANES), 'seq').reshape(-1, LANES)  20 us
    ppermute x1, starting transfers between devices, body(): got = lax.ppermute(projected, 'core', swap)  1.91 us
    pallas_call x1, Pallas kernels, lane_gains(): pl.pallas_call(gain_kernel, out_shape=jax.ShapeDtypeStruct((1, LANES), jn...  1.39 us
  transfers between devices with their start and end apart: 1, of which 1 were waited for; matrix products, arithmetic and copies ran while one was open for 0% of the time, Pallas kernels for 2%

profile of v6, /device:TPU:8, one launch (start us, length us, event | category | flops | bytes accessed | tf_op | source)
XLA Modules:
  0.0 68.7 jit_solution(4644148280288143414)
XLA Ops:
  0.0 1.9 %collective-permute-start = (bf16[3,64,1024]{2,1,0:T(8,128)(2,1)}, bf16[3,64,1024]{2,1,0:T(8,128)(2,1)S(1)}, u32[]{:S(2)}, u32[]{:S(2)}) collective-permute-start(bf16[3,64,1024]{2,1,0:T(8,128)(2,1)} %own_ref.1), channel_id=1, source_target_pairs={{0,1},{1,0},{2,3},{3,2},{4,5},{5,4},{6,7},{7,6},{8,9},{9,8},{10,11... | collective-permute-start | bytes 1179656 | tf_op jit(solution)/shard_map/ppermute | solution.py:314
  1.9 0.0 copy-start
  1.9 0.0 copy-start.1
  1.9 0.0 copy-start.2
  1.9 0.0 copy-start.3
  2.0 1.4 %lane_gains.1.gain_ref = f32[1,128]{1,0:T(1,128)} custom-call(f32[1,16]{1,0:T(1,128)} %bitcast.11), custom_call_target="tpu_custom_call" | custom-call | flops 6000000000 | bytes 20000000 | tf_op jit(solution)/shard_map/lane_gains/pallas_call | solution.py:57
  3.4 0.0 copy-start.4
  3.4 0.5 collective-permute-done.got_ref
  3.8 0.0 copy-done
  3.8 0.0 copy-done.1
  3.8 0.0 copy-done.2
  3.8 0.0 copy-done.3
  3.8 1.4 %forward_blocks.1 = (bf16[1536,128]{1,0:T(8,128)(2,1)S(1)}, bf16[2,16,1024]{2,1,0:T(8,128)(2,1)S(1)}) custom-call(s32[1,32]{1,0:T(1,128)S(1)} %bitcast.10, bf16[3,64,1024]{2,1,0:T(8,128)(2,1)S(1)} %copy-done.1, bf16[3,64,1024]{2,1,0:T(8,128)(2,1)S(1)} %collective-permute-done.got_ref, f32[1,4096]{1,0:T(1,128)S(1)} %copy-done.2, bf16[2,512,1024]{2,1,0:T(8,128)(2,1)S(1)} %copy-done), custom_call_target="tpu_custom_call" | custom-call | tf_op jit(solution)/shard_map/forward_blocks/pallas_call | solution.py:160
  5.2 41.0 %all_to_all.10 = bf16[768,2,128]{2,1,0:T(2,128)(2,1)S(1)} all-to-all(bf16[768,2,128]{2,1,0:T(2,128)(2,1)S(1)} %bitcast.7), channel_id=1, replica_groups=mesh['seq'=128,'yh'=2,'core'=2] {'seq','yh'}, dimensions={0} | all-to-all | bytes 786432 | tf_op jit(solution)/shard_map/all_to_all | solution.py:317
  46.2 0.0 copy-done.4
  46.2 1.3 %mix_blocks.1 = bf16[1280,128]{1,0:T(8,128)(2,1)S(1)} custom-call(bf16[1536,128]{1,0:T(8,128)(2,1)S(1)} %bitcast.8, f32[1,128]{1,0:T(1,128)S(1)} %copy-done.4), custom_call_target="tpu_custom_call" | custom-call | flops 6000000000 | bytes 20000000 | tf_op jit(solution)/shard_map/mix_blocks/pallas_call | solution.py:253
  47.5 20.0 %all_to_all.11 = bf16[640,2,128]{2,1,0:T(2,128)(2,1)S(1)} all-to-all(bf16[640,2,128]{2,1,0:T(2,128)(2,1)S(1)} %bitcast.9), channel_id=1, replica_groups=mesh['seq'=128,'yh'=2,'core'=2] {'seq'}, dimensions={0} | all-to-all | bytes 655360 | tf_op jit(solution)/shard_map/all_to_all | solution.py:319
  67.5 1.2 %inverse_blocks.1 = bf16[16,4096]{1,0:T(8,128)(2,1)} custom-call(bf16[1280,128]{1,0:T(8,128)(2,1)S(1)} %bitcast.6, bf16[2,16,1024]{2,1,0:T(8,128)(2,1)S(1)} %get-tuple-element.12.gate_ref, bf16[2,512,1024]{2,1,0:T(8,128)(2,1)S(1)} %copy-done), custom_call_target="tpu_custom_call" | custom-call | tf_op jit(solution)/shard_map/inverse_blocks/pallas_call | solution.py:299
Async XLA Ops:
  0.0 3.8 %collective-permute-start = (bf16[3,64,1024]{2,1,0:T(8,128)(2,1)}, bf16[3,64,1024]{2,1,0:T(8,128)(2,1)S(1)}, u32[]{:S(2)}, u32[]{:S(2)}) collective-permute-start(bf16[3,64,1024]{2,1,0:T(8,128)(2,1)} %own_ref.1), channel_id=1, source_target_pairs={{0,1},{1,0},{2,3},{3,2},{4,5},{5,4},{6,7},{7,6},{8,9},{9,8},{10,11... | collective-permute-start | bytes 1179656 | tf_op jit(solution)/shard_map/ppermute | solution.py:314
  1.9 1.9 %copy-start = (bf16[2,512,1024]{2,1,0:T(8,128)(2,1)S(1)}, bf16[2,512,1024]{2,1,0:T(8,128)(2,1)}, u32[]{:S(2)}) copy-start(bf16[2,512,1024]{2,1,0:T(8,128)(2,1)} %constant.2.clone.wave) | copy-start | bytes 6291460
  1.9 1.9 %copy-start.1 = (bf16[3,64,1024]{2,1,0:T(8,128)(2,1)S(1)}, bf16[3,64,1024]{2,1,0:T(8,128)(2,1)}, u32[]{:S(2)}) copy-start(bf16[3,64,1024]{2,1,0:T(8,128)(2,1)} %own_ref.1) | copy-start | bytes 1179652
  1.9 1.9 %copy-start.2 = (f32[1,4096]{1,0:T(1,128)S(1)}, f32[1,4096]{1,0:T(1,128)}, u32[]{:S(2)}) copy-start(f32[1,4096]{1,0:T(1,128)} %taps_ref.1) | copy-start | bytes 49156
  1.9 1.9 %copy-start.3 = (s32[32]{0:T(128)S(1)}, s32[32]{0:T(128)}, u32[]{:S(2)}) copy-start(s32[32]{0:T(128)} %param.6) | copy-start | bytes 388
  3.4 42.9 %copy-start.4 = (f32[1,128]{1,0:T(1,128)S(1)}, f32[1,128]{1,0:T(1,128)}, u32[]{:S(2)}) copy-start(f32[1,128]{1,0:T(1,128)} %lane_gains.1.gain_ref) | copy-start | bytes 1540

commit v7 on v6

--- a/solution.py
+++ b/solution.py
@@ -49,20 +49,25 @@
     return jnp.where(lane_ids(v.shape) < HALF, -turned, turned)
 
 
-def gain_kernel(gain_ref, out_ref):
-    out_ref[...] = jnp.concatenate([gain_ref[...]] * (LANES // GROUP), axis=1)
-
-
-def lane_gains(skip_gain):
+SHIFTS = (2 * LANES, (CHAN - 1) * LANES)
+
+
+def shift_kernel(out_ref):
+    source, target = row_ids(SHIFTS), lane_ids(SHIFTS)
+    place = source % HALF + GROUP * (target // LANES + 1) - jnp.where(source < LANES, 0, HALF)
+    same_part = (source // HALF) % 2 == (target // HALF) % 2
+    out_ref[...] = jnp.where(same_part & (place == target % HALF), 1.0, 0.0).astype(jnp.bfloat16)
+
+
+def shift_matrix():
     return pl.pallas_call(
-        gain_kernel,
-        out_shape=jax.ShapeDtypeStruct((1, LANES), jnp.float32),
-        in_specs=[ON_CHIP],
+        shift_kernel,
+        out_shape=jax.ShapeDtypeStruct(SHIFTS, jnp.bfloat16),
         out_specs=ON_CHIP,
-        compiler_params=pltpu.CompilerParams(vmem_limit_bytes=60 * MIB),
+        compiler_params=pltpu.CompilerParams(vmem_limit_bytes=48 * MIB),
         cost_estimate=COST,
-        name="lane_gains",
-    )(skip_gain.reshape(1, GROUP))
+        name="shift_matrix",
+    )()
 
 
 def gate_pieces(blk):
@@ -172,7 +177,7 @@
     )(live_blocks.reshape(1, -1), own, got, taps, wave)
 
 
-def mix_kernel(in_ref, gain_ref, out_ref, spread, wide):
+def mix_kernel(in_ref, gain_ref, shift_ref, out_ref, spread, wide):
     spread[pl.ds(0, SEQ * PAIR), :] = in_ref[...].astype(jnp.float32)
     square = (SEQ, LANES)
     row, lane = row_ids(square), lane_ids(square)
@@ -198,7 +203,7 @@
     before = jnp.where(jnp.concatenate([flip, flip], axis=0), -before, before)
     spec = (turned[:HALF] - before[HALF:], turned[HALF:] + before[:HALF])
     causal = lane <= row
-    gain = gain_ref[...]
+    gain = jnp.concatenate([gain_ref[...]] * (LANES // GROUP), axis=1)
     low_lane = lane % HALF < 2 * GROUP
     signals, rows = [], []
     for k in range(FREQ):
@@ -212,12 +217,7 @@
         signals.append(signal)
         rows.append(jnp.concatenate([signal, late], axis=1).astype(jnp.bfloat16))
     rows = jnp.concatenate(rows, axis=0)
-    shape = (2 * LANES, (CHAN - 1) * LANES)
-    source, target = row_ids(shape), lane_ids(shape)
-    place = source % HALF + GROUP * (target // LANES + 1) - jnp.where(source < LANES, 0, HALF)
-    same_part = (source // HALF) % 2 == (target // HALF) % 2
-    shifts = jnp.where(same_part & (place == target % HALF), 1.0, 0.0).astype(jnp.bfloat16)
-    moved = jnp.dot(rows, shifts, preferred_element_type=jnp.float32).astype(jnp.bfloat16)
+    moved = jnp.dot(rows, shift_ref[...], preferred_element_type=jnp.float32).astype(jnp.bfloat16)
     for k in range(FREQ):
         digit, mirror = k // 2, k % 2
         base = digit * 4 * CHAN + mirror * 2 * CHAN
@@ -249,11 +249,11 @@
     out_ref[...] = wide[pl.ds(0, SEQ * ANSWER), :].astype(jnp.bfloat16)
 
 
-def mix_blocks(received, gain):
+def mix_blocks(received, gain, shifts):
     return pl.pallas_call(
         mix_kernel,
         out_shape=jax.ShapeDtypeStruct((SEQ * ANSWER, LANES), jnp.bfloat16),
-        in_specs=[ON_CHIP, ON_CHIP],
+        in_specs=[ON_CHIP] * 3,
         out_specs=ON_CHIP,
         scratch_shapes=[
             pltpu.VMEM(((SEQ + 1) * PAIR, LANES), jnp.float32),
@@ -262,7 +262,7 @@
         compiler_params=pltpu.CompilerParams(vmem_limit_bytes=48 * MIB),
         cost_estimate=COST,
         name="mix_blocks",
-    )(received, gain)
+    )(received, gain, shifts)
 
 
 def inverse_kernel(spec_ref, gate_ref, wave, out_ref, plain):
@@ -312,10 +312,10 @@
     wave = jnp.asarray(wave_tables())
     swap = ((0, 1), (1, 0))
     got = lax.ppermute(projected, "core", swap)
-    got, gain = lax.optimization_barrier((got, lane_gains(skip_gain)))
+    got, shifts = lax.optimization_barrier((got, shift_matrix()))
     sent, gate = forward_blocks(live_blocks, projected, got, filters, wave)
     got_spec = exchange(sent.reshape(-1, 2, LANES), ("seq", "yh")).reshape(-1, LANES)
-    mixed = mix_blocks(got_spec, gain)
+    mixed = mix_blocks(got_spec, skip_gain.reshape(1, GROUP), shifts)
     spec = exchange(mixed.reshape(-1, 2, LANES), "seq").reshape(-1, LANES)
     return inverse_blocks(spec, gate, wave)
 

time: 68.9 us -> 68.9 us (level)
  waiting for transfers between devices: 0.46 us -> 1.77 us
  Pallas kernels: 5.22 us -> 3.96 us
    ppermute x1, waiting for transfers between devices: 0.46 us -> 1.77 us  [body(): got = lax.ppermute(projected, 'core', swap)]
    pallas_call x1, Pallas kernels: 1.39 us -> 0.11 us  [shift_matrix(): pl.pallas_call(shift_kernel, out_shape=jax.ShapeDtypeStruct(SHIFTS, jnp.b...]
  transfers between devices with their start and end apart: 1 -> 1, of which waited for: 1 -> 1; matrix products, arithmetic and copies ran while one was open for 0% -> 0% of each run, Pallas kernels for 2% -> 0%
where the time goes in v7:
time: 68.9 us; the launch traced here: 68.7 us
  blocking collectives  60.8 us (88%)
  Pallas kernels  3.96 us (6%)
  starting transfers between devices  2.05 us (3%)
  waiting for transfers between devices  1.77 us (3%)
    all_to_all x1, blocking collectives, body(): exchange(sent.reshape(-1, 2, LANES), ('seq', 'yh')).reshape(-1, LANES)  40.9 us
    all_to_all x1, blocking collectives, body(): spec = exchange(mixed.reshape(-1, 2, LANES), 'seq').reshape(-1, LANES)  19.9 us
    ppermute x1, starting transfers between devices, body(): got = lax.ppermute(projected, 'core', swap)  2.05 us
    ppermute x1, waiting for transfers between devices, body(): got = lax.ppermute(projected, 'core', swap)  1.77 us
  transfers between devices with their start and end apart: 1, of which 1 were waited for; matrix products, arithmetic and copies ran while one was open for 0% of the time, Pallas kernels for 0%

profile of v7, /device:TPU:8, one launch (start us, length us, event | category | flops | bytes accessed | tf_op | source)
XLA Modules:
  0.0 68.7 jit_solution(548756302136639236)
XLA Ops:
  0.0 0.0 copy-start
  0.0 0.0 copy-start.1
  0.0 0.0 copy-start.2
  0.0 0.0 copy-start.3
  0.0 2.1 %collective-permute-start = (bf16[3,64,1024]{2,1,0:T(8,128)(2,1)}, bf16[3,64,1024]{2,1,0:T(8,128)(2,1)S(1)}, u32[]{:S(2)}, u32[]{:S(2)}) collective-permute-start(bf16[3,64,1024]{2,1,0:T(8,128)(2,1)} %own_ref.1), channel_id=1, source_target_pairs={{0,1},{1,0},{2,3},{3,2},{4,5},{5,4},{6,7},{7,6},{8,9},{9,8},{10,11... | collective-permute-start | bytes 1179656 | tf_op jit(solution)/shard_map/ppermute | solution.py:314
  2.1 0.1 shift_matrix.1.shift_ref
  2.2 0.0 copy-start.4
  2.2 1.8 %collective-permute-done.got_ref = bf16[3,64,1024]{2,1,0:T(8,128)(2,1)S(1)} collective-permute-done((bf16[3,64,1024]{2,1,0:T(8,128)(2,1)}, bf16[3,64,1024]{2,1,0:T(8,128)(2,1)S(1)}, u32[]{:S(2)}, u32[]{:S(2)}) %collective-permute-start) | collective-permute-done | bytes 393248 | tf_op jit(solution)/shard_map/ppermute | solution.py:314
  4.0 0.0 copy-done
  4.0 0.0 copy-done.1
  4.0 0.0 copy-done.2
  4.0 0.0 copy-done.3
  4.0 1.4 %forward_blocks.1 = (bf16[1536,128]{1,0:T(8,128)(2,1)S(1)}, bf16[2,16,1024]{2,1,0:T(8,128)(2,1)S(1)}) custom-call(s32[1,32]{1,0:T(1,128)S(1)} %bitcast.10, bf16[3,64,1024]{2,1,0:T(8,128)(2,1)S(1)} %copy-done.1, bf16[3,64,1024]{2,1,0:T(8,128)(2,1)S(1)} %collective-permute-done.got_ref, f32[1,4096]{1,0:T(1,128)S(1)} %copy-done.2, bf16[2,512,1024]{2,1,0:T(8,128)(2,1)S(1)} %copy-done), custom_call_target="tpu_custom_call" | custom-call | tf_op jit(solution)/shard_map/forward_blocks/pallas_call | solution.py:165
  5.4 40.9 %all_to_all.10 = bf16[768,2,128]{2,1,0:T(2,128)(2,1)S(1)} all-to-all(bf16[768,2,128]{2,1,0:T(2,128)(2,1)S(1)} %bitcast.7), channel_id=1, replica_groups=mesh['seq'=128,'yh'=2,'core'=2] {'seq','yh'}, dimensions={0} | all-to-all | bytes 786432 | tf_op jit(solution)/shard_map/all_to_all | solution.py:317
  46.3 0.0 copy-done.4
  46.3 1.3 %mix_blocks.1 = bf16[1280,128]{1,0:T(8,128)(2,1)S(1)} custom-call(bf16[1536,128]{1,0:T(8,128)(2,1)S(1)} %bitcast.8, f32[1,16]{1,0:T(1,128)S(1)} %bitcast.11, bf16[256,384]{1,0:T(8,128)(2,1)S(1)} %shift_matrix.1.shift_ref), custom_call_target="tpu_custom_call" | custom-call | flops 6000000000 | bytes 20000000 | tf_op jit(solution)/shard_map/mix_blocks/pallas_call | solution.py:253
  47.6 19.9 %all_to_all.11 = bf16[640,2,128]{2,1,0:T(2,128)(2,1)S(1)} all-to-all(bf16[640,2,128]{2,1,0:T(2,128)(2,1)S(1)} %bitcast.9), channel_id=1, replica_groups=mesh['seq'=128,'yh'=2,'core'=2] {'seq'}, dimensions={0} | all-to-all | bytes 655360 | tf_op jit(solution)/shard_map/all_to_all | solution.py:319
  67.5 1.2 %inverse_blocks.1 = bf16[16,4096]{1,0:T(8,128)(2,1)} custom-call(bf16[1280,128]{1,0:T(8,128)(2,1)S(1)} %bitcast.6, bf16[2,16,1024]{2,1,0:T(8,128)(2,1)S(1)} %get-tuple-element.12.gate_ref, bf16[2,512,1024]{2,1,0:T(8,128)(2,1)S(1)} %copy-done), custom_call_target="tpu_custom_call" | custom-call | tf_op jit(solution)/shard_map/inverse_blocks/pallas_call | solution.py:299
Async XLA Ops:
  0.0 4.0 %copy-start = (bf16[2,512,1024]{2,1,0:T(8,128)(2,1)S(1)}, bf16[2,512,1024]{2,1,0:T(8,128)(2,1)}, u32[]{:S(2)}) copy-start(bf16[2,512,1024]{2,1,0:T(8,128)(2,1)} %constant.2.clone.wave) | copy-start | bytes 6291460
  0.0 4.0 %copy-start.1 = (bf16[3,64,1024]{2,1,0:T(8,128)(2,1)S(1)}, bf16[3,64,1024]{2,1,0:T(8,128)(2,1)}, u32[]{:S(2)}) copy-start(bf16[3,64,1024]{2,1,0:T(8,128)(2,1)} %own_ref.1) | copy-start | bytes 1179652
  0.0 4.0 %copy-start.2 = (f32[1,4096]{1,0:T(1,128)S(1)}, f32[1,4096]{1,0:T(1,128)}, u32[]{:S(2)}) copy-start(f32[1,4096]{1,0:T(1,128)} %taps_ref.1) | copy-start | bytes 49156
  0.0 4.0 %copy-start.3 = (s32[32]{0:T(128)S(1)}, s32[32]{0:T(128)}, u32[]{:S(2)}) copy-start(s32[32]{0:T(128)} %param.6) | copy-start | bytes 388
  0.0 4.0 %collective-permute-start = (bf16[3,64,1024]{2,1,0:T(8,128)(2,1)}, bf16[3,64,1024]{2,1,0:T(8,128)(2,1)S(1)}, u32[]{:S(2)}, u32[]{:S(2)}) collective-permute-start(bf16[3,64,1024]{2,1,0:T(8,128)(2,1)} %own_ref.1), channel_id=1, source_target_pairs={{0,1},{1,0},{2,3},{3,2},{4,5},{5,4},{6,7},{7,6},{8,9},{9,8},{10,11... | collective-permute-start | bytes 1179656 | tf_op jit(solution)/shard_map/ppermute | solution.py:314
  2.2 44.1 %copy-start.4 = (f32[16]{0:T(128)S(1)}, f32[16]{0:T(128)}, u32[]{:S(2)}) copy-start(f32[16]{0:T(128)} %param.8) | copy-start | bytes 196

commit v8 on v6

--- a/solution.py
+++ b/solution.py
@@ -116,9 +116,6 @@
     taps = jnp.concatenate([top, taps - top, top, taps - top], axis=0)
     plain = even | (row_ids((GROUP, BLOCK)) < 2 * CHAN)
     cols[pl.ds(LANES, GROUP), :] = jnp.where(plain, taps, -taps).astype(jnp.bfloat16)
-    cols[pl.ds(LANES + GROUP, LANES - GROUP), :] = jnp.zeros(
-        (LANES - GROUP, BLOCK), jnp.bfloat16
-    )
     weights = cols[...]
     sums = []
     for i in range(2):
@@ -134,6 +131,7 @@
     square = (SEQ, LANES)
     lane = lane_ids(square)
     comb = jnp.zeros(square, jnp.float32)
+    blank = jnp.zeros((SEQ, LANES - GROUP), jnp.float32)
     for i in range(QUAD):
         at = slice(i * SEQ, (i + 1) * SEQ)
         cos, sin = sums[0][at, :LANES], sums[1][at, :LANES]
@@ -142,7 +140,7 @@
         put(MESSAGE + i, jnp.where(lane < HALF, pltpu.roll(cos, HALF, 1), sin))
         for part in range(2):
             move = part * HALF + i * GROUP
-            value = sums[part][at, LANES:]
+            value = jnp.concatenate([sums[part][at, LANES:], blank], axis=1)
             comb = comb + (pltpu.roll(value, move, 1) if move else value)
     comb = jnp.where((lane >= HALF) & ((lane // (2 * CHAN)) % 2 == 1), -comb, comb)
     comb = comb + pltpu.roll(comb, LANES - CHAN, 1)
@@ -163,7 +161,7 @@
         in_specs=[ON_CHIP] * 5,
         out_specs=[ON_CHIP] * 2,
         scratch_shapes=[
-            pltpu.VMEM((2 * LANES, BLOCK), jnp.bfloat16),
+            pltpu.VMEM((LANES + GROUP, BLOCK), jnp.bfloat16),
             pltpu.VMEM(((SEQ + 1) * PAIR, LANES), jnp.float32),
             pltpu.VMEM((2, SEQ + FREQ, LANES), jnp.float32),
         ],

time: 68.9 us -> 68.8 us (level)
  no operation moved by 1% of the time
where the time goes in v8:
time: 68.8 us; the launch traced here: 68.6 us
  blocking collectives  61 us (89%)
  Pallas kernels  5.19 us (8%)
  starting transfers between devices  1.91 us (3%)
    all_to_all x1, blocking collectives, body(): exchange(sent.reshape(-1, 2, LANES), ('seq', 'yh')).reshape(-1, LANES)  41 us
    all_to_all x1, blocking collectives, body(): spec = exchange(mixed.reshape(-1, 2, LANES), 'seq').reshape(-1, LANES)  20 us
    ppermute x1, starting transfers between devices, body(): got = lax.ppermute(projected, 'core', swap)  1.91 us
    pallas_call x1, Pallas kernels, lane_gains(): pl.pallas_call(gain_kernel, out_shape=jax.ShapeDtypeStruct((1, LANES), jn...  1.39 us
  transfers between devices with their start and end apart: 1, of which 1 were waited for; matrix products, arithmetic and copies ran while one was open for 0% of the time, Pallas kernels for 2%

profile of v8, /device:TPU:8, one launch (start us, length us, event | category | flops | bytes accessed | tf_op | source)
XLA Modules:
  0.0 68.6 jit_solution(10816579211003943172)
XLA Ops:
  0.0 1.9 %collective-permute-start = (bf16[3,64,1024]{2,1,0:T(8,128)(2,1)}, bf16[3,64,1024]{2,1,0:T(8,128)(2,1)S(1)}, u32[]{:S(2)}, u32[]{:S(2)}) collective-permute-start(bf16[3,64,1024]{2,1,0:T(8,128)(2,1)} %own_ref.1), channel_id=1, source_target_pairs={{0,1},{1,0},{2,3},{3,2},{4,5},{5,4},{6,7},{7,6},{8,9},{9,8},{10,11... | collective-permute-start | bytes 1179656 | tf_op jit(solution)/shard_map/ppermute | solution.py:312
  1.9 0.0 copy-start
  1.9 0.0 copy-start.1
  1.9 0.0 copy-start.2
  1.9 0.0 copy-start.3
  2.0 1.4 %lane_gains.1.gain_ref = f32[1,128]{1,0:T(1,128)} custom-call(f32[1,16]{1,0:T(1,128)} %bitcast.11), custom_call_target="tpu_custom_call" | custom-call | flops 6000000000 | bytes 20000000 | tf_op jit(solution)/shard_map/lane_gains/pallas_call | solution.py:57
  3.4 0.0 copy-start.4
  3.4 0.5 collective-permute-done.got_ref
  3.8 0.0 copy-done
  3.8 0.0 copy-done.1
  3.8 0.0 copy-done.2
  3.8 0.0 copy-done.3
  3.8 1.3 %forward_blocks.1 = (bf16[1536,128]{1,0:T(8,128)(2,1)S(1)}, bf16[2,16,1024]{2,1,0:T(8,128)(2,1)S(1)}) custom-call(s32[1,32]{1,0:T(1,128)S(1)} %bitcast.10, bf16[3,64,1024]{2,1,0:T(8,128)(2,1)S(1)} %copy-done.1, bf16[3,64,1024]{2,1,0:T(8,128)(2,1)S(1)} %collective-permute-done.got_ref, f32[1,4096]{1,0:T(1,128)S(1)} %copy-done.2, bf16[2,512,1024]{2,1,0:T(8,128)(2,1)S(1)} %copy-done), custom_call_target="tpu_custom_call" | custom-call | tf_op jit(solution)/shard_map/forward_blocks/pallas_call | solution.py:158
  5.2 41.0 %all_to_all.10 = bf16[768,2,128]{2,1,0:T(2,128)(2,1)S(1)} all-to-all(bf16[768,2,128]{2,1,0:T(2,128)(2,1)S(1)} %bitcast.7), channel_id=1, replica_groups=mesh['seq'=128,'yh'=2,'core'=2] {'seq','yh'}, dimensions={0} | all-to-all | bytes 786432 | tf_op jit(solution)/shard_map/all_to_all | solution.py:315
  46.2 0.0 copy-done.4
  46.2 1.3 %mix_blocks.1 = bf16[1280,128]{1,0:T(8,128)(2,1)S(1)} custom-call(bf16[1536,128]{1,0:T(8,128)(2,1)S(1)} %bitcast.8, f32[1,128]{1,0:T(1,128)S(1)} %copy-done.4), custom_call_target="tpu_custom_call" | custom-call | flops 6000000000 | bytes 20000000 | tf_op jit(solution)/shard_map/mix_blocks/pallas_call | solution.py:251
  47.5 20.0 %all_to_all.11 = bf16[640,2,128]{2,1,0:T(2,128)(2,1)S(1)} all-to-all(bf16[640,2,128]{2,1,0:T(2,128)(2,1)S(1)} %bitcast.9), channel_id=1, replica_groups=mesh['seq'=128,'yh'=2,'core'=2] {'seq'}, dimensions={0} | all-to-all | bytes 655360 | tf_op jit(solution)/shard_map/all_to_all | solution.py:317
  67.4 1.2 %inverse_blocks.1 = bf16[16,4096]{1,0:T(8,128)(2,1)} custom-call(bf16[1280,128]{1,0:T(8,128)(2,1)S(1)} %bitcast.6, bf16[2,16,1024]{2,1,0:T(8,128)(2,1)S(1)} %get-tuple-element.12.gate_ref, bf16[2,512,1024]{2,1,0:T(8,128)(2,1)S(1)} %copy-done), custom_call_target="tpu_custom_call" | custom-call | tf_op jit(solution)/shard_map/inverse_blocks/pallas_call | solution.py:297
Async XLA Ops:
  0.0 3.8 %collective-permute-start = (bf16[3,64,1024]{2,1,0:T(8,128)(2,1)}, bf16[3,64,1024]{2,1,0:T(8,128)(2,1)S(1)}, u32[]{:S(2)}, u32[]{:S(2)}) collective-permute-start(bf16[3,64,1024]{2,1,0:T(8,128)(2,1)} %own_ref.1), channel_id=1, source_target_pairs={{0,1},{1,0},{2,3},{3,2},{4,5},{5,4},{6,7},{7,6},{8,9},{9,8},{10,11... | collective-permute-start | bytes 1179656 | tf_op jit(solution)/shard_map/ppermute | solution.py:312
  1.9 1.9 %copy-start = (bf16[2,512,1024]{2,1,0:T(8,128)(2,1)S(1)}, bf16[2,512,1024]{2,1,0:T(8,128)(2,1)}, u32[]{:S(2)}) copy-start(bf16[2,512,1024]{2,1,0:T(8,128)(2,1)} %constant.2.clone.wave) | copy-start | bytes 6291460
  1.9 1.9 %copy-start.1 = (bf16[3,64,1024]{2,1,0:T(8,128)(2,1)S(1)}, bf16[3,64,1024]{2,1,0:T(8,128)(2,1)}, u32[]{:S(2)}) copy-start(bf16[3,64,1024]{2,1,0:T(8,128)(2,1)} %own_ref.1) | copy-start | bytes 1179652
  1.9 1.9 %copy-start.2 = (f32[1,4096]{1,0:T(1,128)S(1)}, f32[1,4096]{1,0:T(1,128)}, u32[]{:S(2)}) copy-start(f32[1,4096]{1,0:T(1,128)} %taps_ref.1) | copy-start | bytes 49156
  1.9 1.9 %copy-start.3 = (s32[32]{0:T(128)S(1)}, s32[32]{0:T(128)}, u32[]{:S(2)}) copy-start(s32[32]{0:T(128)} %param.6) | copy-start | bytes 388
  3.4 42.8 %copy-start.4 = (f32[1,128]{1,0:T(1,128)S(1)}, f32[1,128]{1,0:T(1,128)}, u32[]{:S(2)}) copy-start(f32[1,128]{1,0:T(1,128)} %lane_gains.1.gain_ref) | copy-start | bytes 1540

commit v9 on v6

--- a/solution.py
+++ b/solution.py
@@ -197,8 +197,9 @@
     flip = (half_row // (4 * CHAN) + half_row // (2 * CHAN)) % 2 == 1
     before = jnp.where(jnp.concatenate([flip, flip], axis=0), -before, before)
     spec = (turned[:HALF] - before[HALF:], turned[HALF:] + before[:HALF])
+    spec = [part * (1.0 / BLOCK) for part in spec]
     causal = lane <= row
-    gain = gain_ref[...]
+    gain = gain_ref[...] * (1.0 / BLOCK)
     low_lane = lane % HALF < 2 * GROUP
     signals, rows = [], []
     for k in range(FREQ):
@@ -292,7 +293,7 @@
         ]
         other = jnp.concatenate(other, axis=1)
         gate = jnp.where(high == p // 2, gate_ref[p % 2].astype(jnp.float32), other)
-        out_ref[:, pl.ds(p * BLOCK, BLOCK)] = (gate * (value * (1.0 / BLOCK))).astype(jnp.bfloat16)
+        out_ref[:, pl.ds(p * BLOCK, BLOCK)] = (gate * value).astype(jnp.bfloat16)
 
 
 def inverse_blocks(spec, gate, wave):

time: 68.9 us -> 68.9 us (level)
  no operation moved by 1% of the time
where the time goes in v9:
time: 68.9 us; the launch traced here: 68.7 us
  blocking collectives  61 us (89%)
  Pallas kernels  5.23 us (8%)
  starting transfers between devices  1.91 us (3%)
    all_to_all x1, blocking collectives, body(): exchange(sent.reshape(-1, 2, LANES), ('seq', 'yh')).reshape(-1, LANES)  41 us
    all_to_all x1, blocking collectives, body(): spec = exchange(mixed.reshape(-1, 2, LANES), 'seq').reshape(-1, LANES)  20 us
    ppermute x1, starting transfers between devices, body(): got = lax.ppermute(projected, 'core', swap)  1.91 us
    pallas_call x1, Pallas kernels, lane_gains(): pl.pallas_call(gain_kernel, out_shape=jax.ShapeDtypeStruct((1, LANES), jn...  1.39 us
  transfers between devices with their start and end apart: 1, of which 1 were waited for; matrix products, arithmetic and copies ran while one was open for 0% of the time, Pallas kernels for 2%

profile of v9, /device:TPU:8, one launch (start us, length us, event | category | flops | bytes accessed | tf_op | source)
XLA Modules:
  0.0 68.7 jit_solution(7888792330493599687)
XLA Ops:
  0.0 1.9 %collective-permute-start = (bf16[3,64,1024]{2,1,0:T(8,128)(2,1)}, bf16[3,64,1024]{2,1,0:T(8,128)(2,1)S(1)}, u32[]{:S(2)}, u32[]{:S(2)}) collective-permute-start(bf16[3,64,1024]{2,1,0:T(8,128)(2,1)} %own_ref.1), channel_id=1, source_target_pairs={{0,1},{1,0},{2,3},{3,2},{4,5},{5,4},{6,7},{7,6},{8,9},{9,8},{10,11... | collective-permute-start | bytes 1179656 | tf_op jit(solution)/shard_map/ppermute | solution.py:315
  1.9 0.0 copy-start
  1.9 0.0 copy-start.1
  1.9 0.0 copy-start.2
  1.9 0.0 copy-start.3
  2.0 1.4 %lane_gains.1.gain_ref = f32[1,128]{1,0:T(1,128)} custom-call(f32[1,16]{1,0:T(1,128)} %bitcast.11), custom_call_target="tpu_custom_call" | custom-call | flops 6000000000 | bytes 20000000 | tf_op jit(solution)/shard_map/lane_gains/pallas_call | solution.py:57
  3.4 0.0 copy-start.4
  3.4 0.5 collective-permute-done.got_ref
  3.8 0.0 copy-done
  3.8 0.0 copy-done.1
  3.8 0.0 copy-done.2
  3.8 0.0 copy-done.3
  3.8 1.4 %forward_blocks.1 = (bf16[1536,128]{1,0:T(8,128)(2,1)S(1)}, bf16[2,16,1024]{2,1,0:T(8,128)(2,1)S(1)}) custom-call(s32[1,32]{1,0:T(1,128)S(1)} %bitcast.10, bf16[3,64,1024]{2,1,0:T(8,128)(2,1)S(1)} %copy-done.1, bf16[3,64,1024]{2,1,0:T(8,128)(2,1)S(1)} %collective-permute-done.got_ref, f32[1,4096]{1,0:T(1,128)S(1)} %copy-done.2, bf16[2,512,1024]{2,1,0:T(8,128)(2,1)S(1)} %copy-done), custom_call_target="tpu_custom_call" | custom-call | tf_op jit(solution)/shard_map/forward_blocks/pallas_call | solution.py:160
  5.2 41.0 %all_to_all.10 = bf16[768,2,128]{2,1,0:T(2,128)(2,1)S(1)} all-to-all(bf16[768,2,128]{2,1,0:T(2,128)(2,1)S(1)} %bitcast.7), channel_id=1, replica_groups=mesh['seq'=128,'yh'=2,'core'=2] {'seq','yh'}, dimensions={0} | all-to-all | bytes 786432 | tf_op jit(solution)/shard_map/all_to_all | solution.py:318
  46.2 0.0 copy-done.4
  46.2 1.3 %mix_blocks.1 = bf16[1280,128]{1,0:T(8,128)(2,1)S(1)} custom-call(bf16[1536,128]{1,0:T(8,128)(2,1)S(1)} %bitcast.8, f32[1,128]{1,0:T(1,128)S(1)} %copy-done.4), custom_call_target="tpu_custom_call" | custom-call | flops 6000000000 | bytes 20000000 | tf_op jit(solution)/shard_map/mix_blocks/pallas_call | solution.py:254
  47.5 20.0 %all_to_all.11 = bf16[640,2,128]{2,1,0:T(2,128)(2,1)S(1)} all-to-all(bf16[640,2,128]{2,1,0:T(2,128)(2,1)S(1)} %bitcast.9), channel_id=1, replica_groups=mesh['seq'=128,'yh'=2,'core'=2] {'seq'}, dimensions={0} | all-to-all | bytes 655360 | tf_op jit(solution)/shard_map/all_to_all | solution.py:320
  67.5 1.2 %inverse_blocks.1 = bf16[16,4096]{1,0:T(8,128)(2,1)} custom-call(bf16[1280,128]{1,0:T(8,128)(2,1)S(1)} %bitcast.6, bf16[2,16,1024]{2,1,0:T(8,128)(2,1)S(1)} %get-tuple-element.12.gate_ref, bf16[2,512,1024]{2,1,0:T(8,128)(2,1)S(1)} %copy-done), custom_call_target="tpu_custom_call" | custom-call | tf_op jit(solution)/shard_map/inverse_blocks/pallas_call | solution.py:300
Async XLA Ops:
  0.0 3.8 %collective-permute-start = (bf16[3,64,1024]{2,1,0:T(8,128)(2,1)}, bf16[3,64,1024]{2,1,0:T(8,128)(2,1)S(1)}, u32[]{:S(2)}, u32[]{:S(2)}) collective-permute-start(bf16[3,64,1024]{2,1,0:T(8,128)(2,1)} %own_ref.1), channel_id=1, source_target_pairs={{0,1},{1,0},{2,3},{3,2},{4,5},{5,4},{6,7},{7,6},{8,9},{9,8},{10,11... | collective-permute-start | bytes 1179656 | tf_op jit(solution)/shard_map/ppermute | solution.py:315
  1.9 1.9 %copy-start = (bf16[2,512,1024]{2,1,0:T(8,128)(2,1)S(1)}, bf16[2,512,1024]{2,1,0:T(8,128)(2,1)}, u32[]{:S(2)}) copy-start(bf16[2,512,1024]{2,1,0:T(8,128)(2,1)} %constant.2.clone.wave) | copy-start | bytes 6291460
  1.9 1.9 %copy-start.1 = (bf16[3,64,1024]{2,1,0:T(8,128)(2,1)S(1)}, bf16[3,64,1024]{2,1,0:T(8,128)(2,1)}, u32[]{:S(2)}) copy-start(bf16[3,64,1024]{2,1,0:T(8,128)(2,1)} %own_ref.1) | copy-start | bytes 1179652
  1.9 1.9 %copy-start.2 = (f32[1,4096]{1,0:T(1,128)S(1)}, f32[1,4096]{1,0:T(1,128)}, u32[]{:S(2)}) copy-start(f32[1,4096]{1,0:T(1,128)} %taps_ref.1) | copy-start | bytes 49156
  1.9 1.9 %copy-start.3 = (s32[32]{0:T(128)S(1)}, s32[32]{0:T(128)}, u32[]{:S(2)}) copy-start(s32[32]{0:T(128)} %param.6) | copy-start | bytes 388
  3.4 42.9 %copy-start.4 = (f32[1,128]{1,0:T(1,128)S(1)}, f32[1,128]{1,0:T(1,128)}, u32[]{:S(2)}) copy-start(f32[1,128]{1,0:T(1,128)} %lane_gains.1.gain_ref) | copy-start | bytes 1540
